TPU v7x, 32 devices: a whole 2x2x4 slice. The times are simulated.
32 devices in a mesh: ctx: 16 (over z, y, core), ch: 2 (over x).
Axes of the slice: x: 2, y: 2, z: 4, core: 2. Of those that a mesh axis runs over, the one named last changes fastest.
Arguments:
- streams: bfloat16 [3, 4096, 1024], P(None, 'ctx', 'ch'), may hold values from -6 to 6
- short_weight: float32 [3, 7, 1024], P(None, None, 'ch'), may hold values from -2 to 2
- long_filter: float32 [4096, 1024], P('ctx', 'ch'), may hold values from -32 to 32
- cotangent: bfloat16 [4096, 1024], P('ctx', 'ch'), may hold values from -16 to 16
Outputs:
- hyena_out: bfloat16 [4096, 1024], P('ctx', 'ch')
- stream_grad: bfloat16 [3, 4096, 1024], P(None, 'ctx', 'ch')
- short_grad: float32 [3, 7, 1024], P(None, None, 'ch')
- filter_grad: float32 [4096, 1024], P('ctx', 'ch')
All inputs are finite; a program needn't handle non-finite values.
Results may differ from a plain program's by a relative error of at most 0.0014.
Values may be sent and summed in bfloat16 or wider, within the bound.
A program may use at most 128 MiB of HBM per device.

v0:
```python
import math

import jax
import jax.numpy as jnp
from jax import lax
from jax.sharding import PartitionSpec as P

two_pi = 2.0 * math.pi
highest = lax.Precision.HIGHEST


def passed_along(block, axis, distance):
    devices = range(lax.axis_size(axis))
    route = [(i - distance, i) for i in devices if i - distance in devices]
    return lax.ppermute(block, axis, route)


def phases(left_ints, right_ints, period):
    product = left_ints[:, None] * right_ints[None, :] % period
    return product.astype(jnp.float32) * (two_pi / period)


def group_shape():
    return (lax.axis_size(("ctx", "ch")), lax.axis_index(("ctx", "ch")), lax.axis_size("ch"))


def to_columns(values):
    return lax.all_to_all(values, ("ctx", "ch"), split_axis=4, concat_axis=2, tiled=True)


def to_rows(values):
    return lax.all_to_all(values, ("ctx", "ch"), split_axis=2, concat_axis=4, tiled=True)


def complex_times(left_val, right_val):
    return jnp.stack(
        [
            left_val[0] * right_val[0] - left_val[1] * right_val[1],
            left_val[0] * right_val[1] + left_val[1] * right_val[0],
        ]
    )


def conj_times(left_val, right_val):
    return jnp.stack(
        [
            left_val[0] * right_val[0] + left_val[1] * right_val[1],
            left_val[0] * right_val[1] - left_val[1] * right_val[0],
        ]
    )


def forward_transform(signal):
    members, sequence_index, groups = group_shape()
    signals, block_rows, channels = signal.shape
    blocks = members // groups
    piece_rows = block_rows // members
    period = 2 * blocks * block_rows
    columns = to_columns(signal[None, :, None, None, :, :])
    columns = columns.reshape(signals, blocks, groups, piece_rows, channels)
    coarse = phases(
        jnp.arange(2 * blocks, dtype=jnp.int32), jnp.arange(blocks, dtype=jnp.int32), 2 * blocks
    )
    real_part = jnp.einsum("kp,spgmc->skgmc", jnp.cos(coarse), columns, precision=highest)
    imag_part = -jnp.einsum("kp,spgmc->skgmc", jnp.sin(coarse), columns, precision=highest)
    places = sequence_index * piece_rows + jnp.arange(piece_rows, dtype=jnp.int32)
    twiddle = phases(jnp.arange(2 * blocks, dtype=jnp.int32), places, period)[
        None, :, None, :, None
    ]
    twist_cos = jnp.cos(twiddle)
    twist_sin = jnp.sin(twiddle)
    turned = jnp.stack(
        [
            real_part * twist_cos + imag_part * twist_sin,
            imag_part * twist_cos - real_part * twist_sin,
        ]
    )
    spread = to_rows(turned)
    fine_phase = phases(
        jnp.arange(block_rows, dtype=jnp.int32), jnp.arange(block_rows, dtype=jnp.int32), block_rows
    )
    with_cos = jnp.einsum("zsrgmc,mk->zsrgkc", spread, jnp.cos(fine_phase), precision=highest)
    with_sin = jnp.einsum("zsrgmc,mk->zsrgkc", spread, jnp.sin(fine_phase), precision=highest)
    return jnp.stack([with_cos[0] + with_sin[1], with_cos[1] - with_sin[0]])


def inverse_transform(spectrum):
    members, sequence_index, groups = group_shape()
    signals = spectrum.shape[1]
    freq_rows = spectrum.shape[2]
    block_rows = spectrum.shape[4]
    channels = spectrum.shape[5]
    blocks = members // groups
    piece_rows = block_rows // members
    period = 2 * blocks * block_rows
    fine_phase = phases(
        jnp.arange(block_rows, dtype=jnp.int32), jnp.arange(block_rows, dtype=jnp.int32), block_rows
    )
    with_cos = jnp.einsum("zsrgkc,km->zsrgmc", spectrum, jnp.cos(fine_phase), precision=highest)
    with_sin = jnp.einsum("zsrgkc,km->zsrgmc", spectrum, jnp.sin(fine_phase), precision=highest)
    real_part = with_cos[0] - with_sin[1]
    imag_part = with_cos[1] + with_sin[0]
    freqs = sequence_index * freq_rows + jnp.arange(freq_rows, dtype=jnp.int32)
    twiddle = phases(freqs, jnp.arange(block_rows, dtype=jnp.int32), period)[None, :, None, :, None]
    twist_cos = jnp.cos(twiddle)
    twist_sin = jnp.sin(twiddle)
    turned = jnp.stack(
        [
            real_part * twist_cos - imag_part * twist_sin,
            imag_part * twist_cos + real_part * twist_sin,
        ]
    )
    columns = to_columns(turned)
    coarse = phases(
        jnp.arange(2 * blocks, dtype=jnp.int32), jnp.arange(blocks, dtype=jnp.int32), 2 * blocks
    )
    summed = jnp.einsum("kp,skgmc->spgmc", jnp.cos(coarse), columns[0], precision=highest)
    summed = summed - jnp.einsum("kp,skgmc->spgmc", jnp.sin(coarse), columns[1], precision=highest)
    summed = summed * (1.0 / period)
    gathered = to_rows(summed.reshape(1, signals, members, 1, piece_rows, channels))
    return gathered.reshape(signals, block_rows, channels)


def on_device(streams, short_weight, long_filter, cotangent):
    kernel_len = short_weight.shape[1]
    block_rows = streams.shape[1]
    norm_factor = 1.0 / math.sqrt(block_rows * lax.axis_size("ctx"))
    previous = passed_along(streams[:, block_rows - (kernel_len - 1) :, :], "ctx", 1)
    extended = jnp.concatenate([previous, streams], axis=1)
    features = jnp.zeros(streams.shape, jnp.float32)
    for offset in range(kernel_len):
        start = kernel_len - 1 - offset
        features = (
            features + short_weight[:, offset, None, :] * extended[:, start : start + block_rows, :]
        )
    product = features[1] * features[2]
    scaled = long_filter * norm_factor
    grad_out = cotangent.astype(jnp.float32)
    grad_long = grad_out * features[0]
    spectra = forward_transform(jnp.stack([product, scaled]))
    mixed_long = inverse_transform(complex_times(spectra[:, 0:1], spectra[:, 1:2]))[0]
    grad_spec = forward_transform(grad_long[None])
    kept_product = spectra[:, 0:1]
    kept_filter = spectra[:, 1:2]
    returned = inverse_transform(
        jnp.concatenate(
            [conj_times(kept_filter, grad_spec), conj_times(kept_product, grad_spec)], axis=1
        )
    )
    grad_product = returned[0]
    filter_grad = returned[1] * norm_factor
    hyena_out = (features[0] * mixed_long).astype(jnp.bfloat16)
    grad_query = grad_out * mixed_long
    feature_grad = jnp.stack([grad_query, grad_product * features[2], grad_product * features[1]])
    following = passed_along(
        feature_grad[:, : kernel_len - 1, :].astype(jnp.bfloat16), "ctx", -1
    ).astype(jnp.float32)
    grad_ext = jnp.concatenate([feature_grad, following], axis=1)
    stream_grad = jnp.zeros(feature_grad.shape, jnp.float32)
    short_parts = []
    for offset in range(kernel_len):
        stream_grad = (
            stream_grad
            + short_weight[:, offset, None, :] * grad_ext[:, offset : offset + block_rows, :]
        )
        start = kernel_len - 1 - offset
        short_parts.append(
            jnp.sum(feature_grad * extended[:, start : start + block_rows, :], axis=1)
        )
    short_grad = lax.psum(jnp.stack(short_parts, axis=1), "ctx")
    return (hyena_out, stream_grad.astype(jnp.bfloat16), short_grad, filter_grad)


def solution(mesh):
    placed = (P(None, "ctx", "ch"), P(None, None, "ch"), P("ctx", "ch"), P("ctx", "ch"))
    return jax.shard_map(
        on_device,
        mesh=mesh,
        in_specs=placed,
        out_specs=(P("ctx", "ch"), P(None, "ctx", "ch"), P(None, None, "ch"), P("ctx", "ch")),
        check_vma=False,
    )
```

profile of v0, /device:TPU:0, one launch (start us, length us, event | category | flops | bytes accessed | tf_op | source)
XLA Modules:
  0.0 537.9 jit_solution(11072116281011579739)
XLA Ops:
  7.0 5.6 %fusion.21 = f32[3,256,512]{2,0,1:T(4,128)S(1)} fusion(f32[3,512]{1,0:T(4,128)S(1)} %get-tuple-element.61, f32[3,512]{1,0:T(4,128)S(1)} %get-tuple-element.62, f32[3,512]{1,0:T(4,128)S(1)} %get-tuple-element.63, f32[3,512]{1,0:T(4,128)S(1)} %get-tuple-element.64, f32[3,512]{1,0:T(4,128)S(1)} %get-tuple-element.65, f32[3,512]{1,0:T(4,128)S(1)} %get-tuple-element.66, ...), kind=kLoop, calls=%fused_computation.36 | loop fusion | flops 7864320 | bytes 7120896 | tf_op jit(solution)/shard_map/add | solution.py:134
  17.2 8.8 %all-to-all-start.4 = ((f32[1,1,1,1,256,512]{5,3,2,1,0,4:T(1,128)}), f32[1,1,1,1,256,512]{5,3,2,1,0,4:T(1,128)S(1)}, u32[]{:S(2)}, u32[]{:S(2)}) async-start(f32[1,1,1,1,256,512]{5,3,2,1,0,4:T(1,128)} %copy.56), calls=%async_computation.4 | async-start | bytes 1048576 | tf_op jit(solution)/shard_map/all_to_all | solution.py:28
  28.4 12.7 %all-to-all-done.4 = f32[1,1,1,1,256,512]{5,3,2,1,0,4:T(1,128)S(1)} async-done(((f32[1,1,1,1,256,512]{5,3,2,1,0,4:T(1,128)}), f32[1,1,1,1,256,512]{5,3,2,1,0,4:T(1,128)S(1)}, u32[]{:S(2)}, u32[]{:S(2)}) %all-to-all-start.4) | async-done | bytes 524320 | tf_op jit(solution)/shard_map/all_to_all | solution.py:28
  41.0 3.6 all-to-all-start
  50.6 20.3 %all-to-all-done = f32[1,2,1,1,256,512]{5,1,3,2,0,4:T(2,128)S(1)} async-done(((f32[1,2,1,1,256,512]{5,1,3,2,0,4:T(2,128)}), f32[1,2,1,1,256,512]{5,1,3,2,0,4:T(2,128)S(1)}, u32[]{:S(2)}, u32[]{:S(2)}) %all-to-all-start) | async-done | bytes 1048608 | tf_op jit(solution)/shard_map/all_to_all | solution.py:28
  71.9 3.8 all-to-all-start.5
  79.6 3.0 fusion.43
  83.4 4.4 copy.49
  87.8 36.6 %all-to-all-done.5 = f32[2,1,32,2,8,512]{5,4,3,1,0,2:T(8,128)S(1)} async-done(((f32[2,1,32,2,8,512]{5,4,3,1,0,2:T(8,128)}), f32[2,1,32,2,8,512]{5,4,3,1,0,2:T(8,128)S(1)}, u32[]{:S(2)}, u32[]{:S(2)}) %all-to-all-start.5) | async-done | bytes 2097184 | tf_op jit(solution)/shard_map/all_to_all | solution.py:32
  124.4 4.2 all-to-all-start.1
  128.7 4.2 fusion.55
  132.9 4.2 fusion.52
  137.1 85.2 %all-to-all-done.1 = f32[2,2,32,2,8,512]{5,4,3,1,0,2:T(8,128)} async-done(((f32[2,2,32,2,8,512]{5,4,3,1,0,2:T(8,128)}), f32[2,2,32,2,8,512]{5,4,3,1,0,2:T(8,128)}, u32[]{:S(2)}, u32[]{:S(2)}) %all-to-all-start.1) | async-done | bytes 4194336 | tf_op jit(solution)/shard_map/all_to_all | solution.py:32
  222.4 7.5 %fusion.13 = f32[2,2,1,2,256,512]{5,4,3,1,0,2:T(8,128)S(1)} fusion(f32[2,2,32,2,8,512]{5,4,3,1,0,2:T(8,128)} %all-to-all-done.1), kind=kOutput, calls=%fused_computation.29 | convolution fusion | flops 3222142976 | bytes 8388608 | tf_op jit(solution)/shard_map/zsrgmc,mk->zsrgkc/dot_general | solution.py:83
  229.9 7.7 %fusion.10 = f32[2,2,1,2,256,512]{5,4,3,1,0,2:T(8,128)S(1)} fusion(f32[2,2,32,2,8,512]{5,4,3,1,0,2:T(8,128)} %all-to-all-done.1), kind=kOutput, calls=%fused_computation.28 | convolution fusion | flops 3222142976 | bytes 8388608 | tf_op jit(solution)/shard_map/zsrgmc,mk->zsrgkc/dot_general | solution.py:82
  250.6 3.0 copy.51
  253.6 5.2 all-to-all-start.2
  258.8 7.3 %fusion.9 = f32[2,2,1,2,256,512]{5,4,3,1,0,2:T(8,128)S(1)} fusion(f32[1,1,1,2,256,512]{5,4,3,1,0,2:T(8,128)} %get-tuple-element.32, f32[1,1,1,2,256,512]{5,4,3,1,0,2:T(8,128)} %get-tuple-element.31, f32[1,1,1,2,256,512]{5,4,3,1,0,2:T(8,128)} %get-tuple-element.30, f32[1,1,1,2,256,512]{5,4,3,1,0,2:T(8,128)} %get-tuple-element.23), kind=kOutput, calls=%fused_computation.27 | convolution fusion | flops 3225288704 | bytes 8388608 | tf_op jit(solution)/shard_map/zsrgkc,km->zsrgmc/dot_general | solution.py:100
  266.2 5.1 fusion.8
  273.0 5.4 copy.61
  278.4 28.7 %all-to-all-done.2 = f32[2,1,1,2,256,512]{5,3,0,2,1,4:T(2,128)S(1)} async-done(((f32[2,1,1,2,256,512]{5,3,0,2,1,4:T(2,128)}), f32[2,1,1,2,256,512]{5,3,0,2,1,4:T(2,128)S(1)}, u32[]{:S(2)}, u32[]{:S(2)}) %all-to-all-start.2) | async-done | bytes 2097184 | tf_op jit(solution)/shard_map/all_to_all | solution.py:28
  307.1 3.8 all-to-all-start.6
  314.7 89.9 %all-to-all-done.6 = f32[2,2,1,2,256,512]{5,3,1,0,2,4:T(2,128)} async-done(((f32[2,2,1,2,256,512]{5,3,1,0,2,4:T(2,128)}), f32[2,2,1,2,256,512]{5,3,1,0,2,4:T(2,128)}, u32[]{:S(2)}, u32[]{:S(2)}) %all-to-all-start.6) | async-done | bytes 4194336 | tf_op jit(solution)/shard_map/all_to_all | solution.py:28
  404.6 4.7 all-to-all-start.3
  409.4 4.6 copy.141
  418.4 6.0 %all-to-all-done.3 = f32[1,1,32,1,8,512]{5,4,3,1,0,2:T(8,128)S(1)} async-done(((f32[1,1,32,1,8,512]{5,4,3,1,0,2:T(8,128)}), f32[1,1,32,1,8,512]{5,4,3,1,0,2:T(8,128)S(1)}, u32[]{:S(2)}, u32[]{:S(2)}) %all-to-all-start.3) | async-done | bytes 524320 | tf_op jit(solution)/shard_map/all_to_all | solution.py:32
  424.4 3.6 all-to-all-start.7
  429.4 24.8 %all-to-all-done.7 = f32[1,2,32,1,8,512]{5,4,1,3,0,2:T(8,128)S(1)} async-done(((f32[1,2,32,1,8,512]{5,4,1,3,0,2:T(8,128)}), f32[1,2,32,1,8,512]{5,4,1,3,0,2:T(8,128)S(1)}, u32[]{:S(2)}, u32[]{:S(2)}) %all-to-all-start.7) | async-done | bytes 1048608 | tf_op jit(solution)/shard_map/all_to_all | solution.py:32
  457.1 3.6 slice_multiply_fusion.7
  462.2 5.3 fusion.28
  470.0 60.7 %psum.7 = f32[3,7,512]{2,0,1:T(4,128)S(1)} all-reduce(f32[3,7,512]{2,0,1:T(4,128)S(1)} %constant_dynamic-update-slice_fusion.2), channel_id=1, replica_groups=mesh['ctx'=16,'ch'=2] {'ctx'}, use_global_device_ids=true, to_apply=%region_7.8 | all-reduce | flops 10752 | bytes 86016 | tf_op jit(solution)/shard_map/psum | solution.py:170
  532.8 3.8 fusion.30
  (97 shorter events, 58.9 us)
Async XLA Ops:
  0.6 6.4 %copy-start.3 = (bf16[3,256,512]{2,1,0:T(8,128)(2,1)S(1)}, bf16[3,256,512]{2,1,0:T(8,128)(2,1)}, u32[]{:S(2)}) copy-start(bf16[3,256,512]{2,1,0:T(8,128)(2,1)} %param.4) | copy-start | bytes 2359300
  1.5 3.6 collective-permute-start
  12.6 1.4 copy-start
  14.0 1.8 copy-start.11
  15.0 0.8 copy-start.5
  15.0 11.0 %copy-start.15 = (f32[256,512]{1,0:T(8,128)S(1)}, f32[256,512]{1,0:T(8,128)}, u32[]{:S(2)}) copy-start(f32[256,512]{1,0:T(8,128)} %param.6) | copy-start | bytes 1572868
  17.2 23.8 %all-to-all-start.4 = ((f32[1,1,1,1,256,512]{5,3,2,1,0,4:T(1,128)}), f32[1,1,1,1,256,512]{5,3,2,1,0,4:T(1,128)S(1)}, u32[]{:S(2)}, u32[]{:S(2)}) async-start(f32[1,1,1,1,256,512]{5,3,2,1,0,4:T(1,128)} %copy.56), calls=%async_computation.4 | async-start | bytes 1048576 | tf_op jit(solution)/shard_map/all_to_all | solution.py:28
  41.0 29.9 %all-to-all-start = ((f32[1,2,1,1,256,512]{5,1,3,2,0,4:T(2,128)}), f32[1,2,1,1,256,512]{5,1,3,2,0,4:T(2,128)S(1)}, u32[]{:S(2)}, u32[]{:S(2)}) async-start(f32[1,2,1,1,256,512]{5,1,3,2,0,4:T(2,128)} %maximum_bitcast_fusion.14), calls=%async_computation | async-start | bytes 2097152 | tf_op jit(solution)/shard_map/all_to_all | solution.py:28
  70.9 1.0 copy-start.9
  71.9 52.5 %all-to-all-start.5 = ((f32[2,1,32,2,8,512]{5,4,3,1,0,2:T(8,128)}), f32[2,1,32,2,8,512]{5,4,3,1,0,2:T(8,128)S(1)}, u32[]{:S(2)}, u32[]{:S(2)}) async-start(f32[2,1,32,2,8,512]{5,4,3,1,0,2:T(8,128)} %copy.59), calls=%async_computation.5 | async-start | bytes 4194304 | tf_op jit(solution)/shard_map/all_to_all | solution.py:32
  124.4 97.9 %all-to-all-start.1 = ((f32[2,2,32,2,8,512]{5,4,3,1,0,2:T(8,128)}), f32[2,2,32,2,8,512]{5,4,3,1,0,2:T(8,128)}, u32[]{:S(2)}, u32[]{:S(2)}) async-start(f32[2,2,32,2,8,512]{5,4,3,1,0,2:T(8,128)} %copy.49), calls=%async_computation.1 | async-start | bytes 8388608 | tf_op jit(solution)/shard_map/all_to_all | solution.py:32
  237.6 1.6 copy-start.1
  237.6 2.2 copy-start.2
  253.6 53.5 %all-to-all-start.2 = ((f32[2,1,1,2,256,512]{5,3,0,2,1,4:T(2,128)}), f32[2,1,1,2,256,512]{5,3,0,2,1,4:T(2,128)S(1)}, u32[]{:S(2)}, u32[]{:S(2)}) async-start(f32[2,1,1,2,256,512]{5,3,0,2,1,4:T(2,128)} %copy.51), calls=%async_computation.2 | async-start | bytes 4194304 | tf_op jit(solution)/shard_map/all_to_all | solution.py:28
  258.8 7.4 %copy-start.10 = (f32[1,1,1,2,256,512]{5,4,3,1,0,2:T(8,128)S(1)}, f32[1,1,1,2,256,512]{5,4,3,1,0,2:T(8,128)}, u32[]{:S(2)}) copy-start(f32[1,1,1,2,256,512]{5,4,3,1,0,2:T(8,128)} %get-tuple-element.23) | copy-start | bytes 3145732
  258.8 7.4 %copy-start.12 = (f32[1,1,1,2,256,512]{5,4,3,1,0,2:T(8,128)S(1)}, f32[1,1,1,2,256,512]{5,4,3,1,0,2:T(8,128)}, u32[]{:S(2)}) copy-start(f32[1,1,1,2,256,512]{5,4,3,1,0,2:T(8,128)} %get-tuple-element.30) | copy-start | bytes 3145732
  258.8 7.4 %copy-start.13 = (f32[1,1,1,2,256,512]{5,4,3,1,0,2:T(8,128)S(1)}, f32[1,1,1,2,256,512]{5,4,3,1,0,2:T(8,128)}, u32[]{:S(2)}) copy-start(f32[1,1,1,2,256,512]{5,4,3,1,0,2:T(8,128)} %get-tuple-element.31) | copy-start | bytes 3145732
  258.8 7.4 %copy-start.14 = (f32[1,1,1,2,256,512]{5,4,3,1,0,2:T(8,128)S(1)}, f32[1,1,1,2,256,512]{5,4,3,1,0,2:T(8,128)}, u32[]{:S(2)}) copy-start(f32[1,1,1,2,256,512]{5,4,3,1,0,2:T(8,128)} %get-tuple-element.32) | copy-start | bytes 3145732
  307.1 97.5 %all-to-all-start.6 = ((f32[2,2,1,2,256,512]{5,3,1,0,2,4:T(2,128)}), f32[2,2,1,2,256,512]{5,3,1,0,2,4:T(2,128)}, u32[]{:S(2)}, u32[]{:S(2)}) async-start(f32[2,2,1,2,256,512]{5,3,1,0,2,4:T(2,128)} %copy.61), calls=%async_computation.6 | async-start | bytes 8388608 | tf_op jit(solution)/shard_map/all_to_all | solution.py:28
  404.6 19.7 %all-to-all-start.3 = ((f32[1,1,32,1,8,512]{5,4,3,1,0,2:T(8,128)}), f32[1,1,32,1,8,512]{5,4,3,1,0,2:T(8,128)S(1)}, u32[]{:S(2)}, u32[]{:S(2)}) async-start(f32[1,1,32,1,8,512]{5,4,3,1,0,2:T(8,128)} %bitcast.47), calls=%async_computation.3 | async-start | bytes 1048576 | tf_op jit(solution)/shard_map/all_to_all | solution.py:32
  417.2 10.8 %copy-start.6 = (f32[1,256,512]{2,0,1:T(1,128)S(1)}, f32[1,256,512]{2,0,1:T(1,128)}, u32[]{:S(2)}) copy-start(f32[1,256,512]{2,0,1:T(1,128)} %copy-done.5) | copy-start | bytes 1572868
  424.4 29.9 %all-to-all-start.7 = ((f32[1,2,32,1,8,512]{5,4,1,3,0,2:T(8,128)}), f32[1,2,32,1,8,512]{5,4,1,3,0,2:T(8,128)S(1)}, u32[]{:S(2)}, u32[]{:S(2)}) async-start(f32[1,2,32,1,8,512]{5,4,1,3,0,2:T(8,128)} %copy.65), calls=%async_computation.7 | async-start | bytes 2097152 | tf_op jit(solution)/shard_map/all_to_all | solution.py:32
  454.3 1.2 copy-start.7
  457.1 5.1 copy-start.4
  462.2 7.0 %copy-start.8 = (f32[1,2,32,1,8,512]{5,4,1,3,0,2:T(8,128)S(1)}, f32[1,2,32,1,8,512]{5,4,1,3,0,2:T(8,128)}, u32[]{:S(2)}) copy-start(f32[1,2,32,1,8,512]{5,4,1,3,0,2:T(8,128)} %copy-done.7) | copy-start | bytes 3145732
  467.6 63.8 %collective-permute-start.1 = (bf16[3,6,512]{2,0,1:T(4,128)(2,1)S(1)}, bf16[3,6,512]{2,0,1:T(4,128)(2,1)S(1)}, u32[]{:S(2)}, u32[]{:S(2)}) collective-permute-start(bf16[3,6,512]{2,0,1:T(4,128)(2,1)S(1)} %slice.418), channel_id=1, source_target_pairs={{2,0},{4,2},{6,4},{8,6},{10,8},{12,10},{14,12},{16,14},{18,16},{20... | collective-permute-start | bytes 55304 | tf_op jit(solution)/shard_map/ppermute | solution.py:15
where the time goes:
time: 547 us; the launch traced here: 538 us
  waiting for transfers between devices  304 us (56%)
  blocking collectives  60.7 us (11%)
  matrix products  54.3 us (10%)
  starting transfers between devices  41.7 us (8%)
  local copies, waits for them, and re-layouts  40.5 us (7%)
  other arithmetic  34.8 us (6%)
    all_to_all x4, waiting for transfers between devices, to_rows(): lax.all_to_all(values, ('ctx', 'ch'), split_axis=2, concat_axis=4, tiled=...  153 us
    all_to_all x4, waiting for transfers between devices, to_columns(): lax.all_to_all(values, ('ctx', 'ch'), split_axis=4, concat_axis=2, tiled=...  152 us
    psum x1, blocking collectives, on_device(): short_grad = lax.psum(jnp.stack(short_parts, axis=1), 'ctx')  60.7 us
    all_to_all x4, starting transfers between devices, to_columns(): lax.all_to_all(values, ('ctx', 'ch'), split_axis=4, concat_axis=2, tiled=...  21.4 us
    all_to_all x4, starting transfers between devices, to_rows(): lax.all_to_all(values, ('ctx', 'ch'), split_axis=2, concat_axis=4, tiled=...  16.4 us
    dot_general x2, matrix products, forward_transform(): jnp.einsum('zsrgmc,mk->zsrgkc', spread, jnp.cos(fine_phase), precision=hi...  11.9 us
    dot_general x2, matrix products, forward_transform(): jnp.einsum('zsrgmc,mk->zsrgkc', spread, jnp.sin(fine_phase), precision=hi...  11.8 us
  transfers between devices with their start and end apart: 10, of which 8 were waited for; matrix products, arithmetic and copies ran while one was open for 12% of the time, Pallas kernels for 0%

commit v1 on v0

v1 whole, which is shorter than its diff:
```python
import functools
import math

import jax
import jax.numpy as jnp
import numpy as np
from jax import lax
from jax.experimental import pallas as pl
from jax.experimental.pallas import tpu as pltpu
from jax.sharding import PartitionSpec as P

span = 250.0
half_span = 125.0
tiny = 1e-30
f32 = jnp.float32


def passed_along(block, axis, distance):
    devices = range(lax.axis_size(axis))
    route = [(i - distance, i) for i in devices if i - distance in devices]
    return lax.ppermute(block, axis, route)


def encode(values, top):
    power = jnp.abs(values) * (span / top) - half_span
    code = jnp.exp2(power)
    return jnp.where(values < 0.0, -code, code).astype(jnp.bfloat16)


def decode(code, top):
    code = code.astype(f32)
    size = (jnp.log2(jnp.abs(code)) + half_span) * (top * (1.0 / span))
    return jnp.where(code < 0.0, -size, size)


def row_top(values):
    return jnp.maximum(jnp.max(jnp.abs(values), axis=1, keepdims=True), tiny)


def to_lanes(column):
    rows = column.shape[0]
    lane = lax.broadcasted_iota(jnp.int32, (rows, 128), 1)
    row = lax.broadcasted_iota(jnp.int32, (rows, 128), 0)
    return jnp.sum(jnp.where(lane == row, column, 0.0), axis=0, keepdims=True)


def to_column(line, rows):
    lane = lax.broadcasted_iota(jnp.int32, (rows, 128), 1)
    row = lax.broadcasted_iota(jnp.int32, (rows, 128), 0)
    return jnp.sum(jnp.where(lane == row, line, 0.0), axis=1, keepdims=True)


def three_products(values, high_ref, low_ref):
    high = values.astype(jnp.bfloat16)
    low = (values - high.astype(f32)).astype(jnp.bfloat16)
    dot = functools.partial(jnp.dot, preferred_element_type=f32)
    return dot(high, high_ref[...]) + (dot(low, high_ref[...]) + dot(high, low_ref[...]))


def conv_kernel(
    members, chans, norm, prod_ref, filt_ref, grad_ref, cos_ref, sin_ref, twist_ref,
    fwd_high, fwd_low, inv_high, inv_low, out_ref,
    turned, packed, tops, got, got_tops, back, back_tops, home, home_tops, waves, spectra,
    send_sem, top_send, recv_sem, top_recv, back_send, back_top_send, back_recv, back_top_recv,
):
    me = lax.axis_index("ctx")
    mine = lax.axis_index("ch")
    rows = prod_ref.shape[0]
    half = members // 2

    def target(other):
        return (other, mine)

    barrier = pltpu.get_barrier_semaphore()

    def greet(step, carry):
        other = lax.rem(me + step, members)
        pl.semaphore_signal(
            barrier, inc=1, device_id=target(other), device_id_type=pl.DeviceIdType.MESH
        )
        return carry

    lax.fori_loop(1, members, greet, 0)

    for which, ref in enumerate((prod_ref, filt_ref, grad_ref)):
        turned[which] = ref[...].T

    def pack(other, carry):
        for which in range(3):
            values = turned[which, pl.ds(pl.multiple_of(other * chans, chans), chans), :]
            top = row_top(values)
            packed[other, which] = encode(values, top)
            tops[other, which : which + 1, :] = to_lanes(top)
        return carry

    lax.fori_loop(0, members, pack, 0)
    pl.semaphore_wait(barrier, members - 1)

    def outward(other, source):
        return (
            pltpu.make_async_remote_copy(
                src_ref=packed.at[other], dst_ref=got.at[source],
                send_sem=send_sem.at[other], recv_sem=recv_sem.at[source],
                device_id=target(other), device_id_type=pl.DeviceIdType.MESH,
            ),
            pltpu.make_async_remote_copy(
                src_ref=tops.at[other], dst_ref=got_tops.at[source],
                send_sem=top_send.at[other], recv_sem=top_recv.at[source],
                device_id=target(other), device_id_type=pl.DeviceIdType.MESH,
            ),
        )

    def homeward(other, source):
        return (
            pltpu.make_async_remote_copy(
                src_ref=back.at[other], dst_ref=home.at[source],
                send_sem=back_send.at[other], recv_sem=back_recv.at[source],
                device_id=target(other), device_id_type=pl.DeviceIdType.MESH,
            ),
            pltpu.make_async_remote_copy(
                src_ref=back_tops.at[other], dst_ref=home_tops.at[source],
                send_sem=back_top_send.at[other], recv_sem=back_top_recv.at[source],
                device_id=target(other), device_id_type=pl.DeviceIdType.MESH,
            ),
        )

    def post(step, carry):
        for copy in outward(lax.rem(me + step, members), me):
            copy.start()
        return carry

    lax.fori_loop(1, members, post, 0)
    got[me] = packed[me]
    got_tops[me] = tops[me]

    def unpack(step, carry):
        source = lax.rem(me + members - step, members)

        @pl.when(step > 0)
        def _():
            for copy in outward(source, source):
                copy.wait_recv()

        for which in range(3):
            top = to_column(got_tops[source, which : which + 1, :], chans)
            if which == 1:
                top = top * norm
            waves[which, source] = decode(got[source, which], top)
        return carry

    lax.fori_loop(0, members, unpack, 0)

    def coarse(index, carry):
        which = index // (half + 1)
        freq = lax.rem(index, half + 1)
        sums = []
        for parity in range(2):
            real = jnp.zeros((chans, rows), f32)
            imag = jnp.zeros((chans, rows), f32)
            for block in range(parity, members, 2):
                value = waves[which, block]
                real = real + cos_ref[freq, block] * value
                imag = imag - sin_ref[freq, block] * value
            sums.append((real, imag))
        (er, ei), (odd_r, odd_i) = sums

        def put(place, real, imag):
            cosine = twist_ref[0, pl.ds(place, 1), :]
            sine = twist_ref[1, pl.ds(place, 1), :]
            spectra[which, place, :, :rows] = real * cosine + imag * sine
            spectra[which, place, :, rows:] = imag * cosine - real * sine

        put(members - freq, er - odd_r, odd_i - ei)
        put(freq, er + odd_r, ei + odd_i)
        return carry

    lax.fori_loop(0, 3 * (half + 1), coarse, 0)

    height = (members + 1) * chans

    def fine(which, carry):
        flat = spectra[which].reshape(height, 2 * rows)
        spectra[which] = three_products(flat, fwd_high, fwd_low).reshape(
            members + 1, chans, 2 * rows
        )
        return carry

    lax.fori_loop(0, 3, fine, 0)

    def multiply(freq, carry):
        (pr, pi), (hr, hi), (gr, gi) = [
            (spectra[which, freq, :, :rows], spectra[which, freq, :, rows:]) for which in range(3)
        ]
        spectra[0, freq, :, :rows] = pr * hr - pi * hi
        spectra[0, freq, :, rows:] = pr * hi + pi * hr
        spectra[1, freq, :, :rows] = hr * gr + hi * gi
        spectra[1, freq, :, rows:] = hr * gi - hi * gr
        spectra[2, freq, :, :rows] = pr * gr + pi * gi
        spectra[2, freq, :, rows:] = pr * gi - pi * gr
        return carry

    lax.fori_loop(0, members + 1, multiply, 0)

    def unfine(which, carry):
        flat = spectra[which].reshape(height, 2 * rows)
        spectra[which] = three_products(flat, inv_high, inv_low).reshape(
            members + 1, chans, 2 * rows
        )
        return carry

    lax.fori_loop(0, 3, unfine, 0)

    def untwist(index, carry):
        which = index // (half + 1)
        freq = lax.rem(index, half + 1)

        def turn(place):
            cosine = twist_ref[0, pl.ds(place, 1), :]
            sine = twist_ref[1, pl.ds(place, 1), :]
            real = spectra[which, place, :, :rows]
            imag = spectra[which, place, :, rows:]
            return real * cosine - imag * sine, imag * cosine + real * sine

        lr, li = turn(freq)
        ur, ui = turn(members - freq)
        ones = jnp.where(freq == half, 0.0, 1.0)
        weight = jnp.where(freq == 0, 1.0, 2.0) / (2.0 * members * rows)
        spectra[which, freq, :, :rows] = weight * (lr + ones * ur)
        spectra[which, freq, :, rows:] = weight * (li - ones * ui)

        @pl.when(freq < half)
        def _():
            spectra[which, members - freq, :, :rows] = weight * (lr - ur)
            spectra[which, members - freq, :, rows:] = weight * (li + ui)

        return carry

    lax.fori_loop(0, 3 * (half + 1), untwist, 0)

    def finish(block, odd):
        for which in range(3):
            total = jnp.zeros((chans, rows), f32)
            for freq in range(half + 1):
                place = members - freq if odd else freq
                total = total + cos_ref[freq, block] * spectra[which, place, :, :rows]
                total = total - sin_ref[freq, block] * spectra[which, place, :, rows:]
            if which == 2:
                total = total * norm
            top = row_top(total)
            back[block, which] = encode(total, top)
            back_tops[block, which : which + 1, :] = to_lanes(top)

        @pl.when(block != me)
        def _():
            for copy in homeward(block, me):
                copy.start()

    def finish_pair(pair, carry):
        finish(2 * pair, False)
        finish(2 * pair + 1, True)
        return carry

    lax.fori_loop(0, half, finish_pair, 0)
    home[me] = back[me]
    home_tops[me] = back_tops[me]

    def settle(step, carry):
        source = lax.rem(me + members - step, members)

        @pl.when(step > 0)
        def _():
            for copy in homeward(source, source):
                copy.wait_recv()

        for which in range(3):
            top = to_column(home_tops[source, which : which + 1, :], chans)
            turned[which, pl.ds(pl.multiple_of(source * chans, chans), chans), :] = decode(
                home[source, which], top
            )
        return carry

    lax.fori_loop(0, members, settle, 0)
    for which in range(3):
        out_ref[which] = turned[which].T

    def drain(step, carry):
        other = lax.rem(me + step, members)
        for copy in outward(other, me) + homeward(other, me):
            copy.wait_send()
        return carry

    lax.fori_loop(1, members, drain, 0)


def tables(members, rows):
    period = 2 * members * rows
    coarse = np.outer(np.arange(members // 2 + 1), np.arange(members)) % (2 * members)
    coarse = coarse * (math.pi / members)
    twist = np.outer(np.arange(members + 1), np.arange(rows)) % period * (2.0 * math.pi / period)
    fine = np.outer(np.arange(rows), np.arange(rows)) % rows * (2.0 * math.pi / rows)
    c, s = np.cos(fine), np.sin(fine)
    forward = np.block([[c, -s], [s, c]])

    def split(matrix):
        high = matrix.astype(jnp.bfloat16)
        return high, (matrix - high.astype(np.float64)).astype(jnp.bfloat16)

    return (
        np.cos(coarse).astype(np.float32),
        np.sin(coarse).astype(np.float32),
        np.stack([np.cos(twist), np.sin(twist)]).astype(np.float32),
        *split(forward),
        *split(forward.T),
    )


def convolutions(product, long_filter, grad_long, norm):
    members = lax.axis_size("ctx")
    rows, width = product.shape
    chans = width // members
    vmem = pl.BlockSpec(memory_space=pltpu.VMEM)
    smem = pl.BlockSpec(memory_space=pltpu.SMEM)
    wire = pltpu.VMEM((members, 3, chans, rows), jnp.bfloat16)
    peaks = pltpu.VMEM((members, 8, 128), f32)
    sems = pltpu.SemaphoreType.DMA((members,))
    return pl.pallas_call(
        functools.partial(conv_kernel, members, chans, norm),
        out_shape=jax.ShapeDtypeStruct((3, rows, width), f32),
        in_specs=[vmem] * 3 + [smem] * 2 + [vmem] * 5,
        out_specs=vmem,
        scratch_shapes=[
            pltpu.VMEM((3, width, rows), f32),
            wire, peaks, wire, peaks, wire, peaks, wire, peaks,
            pltpu.VMEM((3, members, chans, rows), f32),
            pltpu.VMEM((3, members + 1, chans, 2 * rows), f32),
        ]
        + [sems] * 8,
        compiler_params=pltpu.CompilerParams(
            collective_id=0, has_side_effects=True, vmem_limit_bytes=48 * 1024 * 1024
        ),
    )(product, long_filter, grad_long, *[jnp.asarray(t) for t in tables(members, rows)])


def on_device(streams, short_weight, long_filter, cotangent):
    kernel_len = short_weight.shape[1]
    block_rows = streams.shape[1]
    norm_factor = 1.0 / math.sqrt(block_rows * lax.axis_size("ctx"))
    previous = passed_along(streams[:, block_rows - (kernel_len - 1) :, :], "ctx", 1)
    extended = jnp.concatenate([previous, streams], axis=1)
    features = jnp.zeros(streams.shape, f32)
    for offset in range(kernel_len):
        start = kernel_len - 1 - offset
        features = (
            features + short_weight[:, offset, None, :] * extended[:, start : start + block_rows, :]
        )
    grad_out = cotangent.astype(f32)
    mixed_long, grad_product, filter_grad = convolutions(
        features[1] * features[2], long_filter, grad_out * features[0], norm_factor
    )
    hyena_out = (features[0] * mixed_long).astype(jnp.bfloat16)
    grad_query = grad_out * mixed_long
    feature_grad = jnp.stack([grad_query, grad_product * features[2], grad_product * features[1]])
    following = passed_along(
        feature_grad[:, : kernel_len - 1, :].astype(jnp.bfloat16), "ctx", -1
    ).astype(f32)
    grad_ext = jnp.concatenate([feature_grad, following], axis=1)
    stream_grad = jnp.zeros(feature_grad.shape, f32)
    short_parts = []
    for offset in range(kernel_len):
        stream_grad = (
            stream_grad
            + short_weight[:, offset, None, :] * grad_ext[:, offset : offset + block_rows, :]
        )
        start = kernel_len - 1 - offset
        short_parts.append(
            jnp.sum(feature_grad * extended[:, start : start + block_rows, :], axis=1)
        )
    short_grad = lax.psum(jnp.stack(short_parts, axis=1), "ctx")
    return (hyena_out, stream_grad.astype(jnp.bfloat16), short_grad, filter_grad)


def solution(mesh):
    placed = (P(None, "ctx", "ch"), P(None, None, "ch"), P("ctx", "ch"), P("ctx", "ch"))
    return jax.shard_map(
        on_device,
        mesh=mesh,
        in_specs=placed,
        out_specs=(P("ctx", "ch"), P(None, "ctx", "ch"), P(None, None, "ch"), P("ctx", "ch")),
        check_vma=False,
    )
```

time: 547 us -> 144 us (0.26); the launches traced: 538 us -> 144 us
  waiting for transfers between devices: 304 us -> 0.01 us
  matrix products: 54.3 us -> 0 us
  Pallas kernels: 0 us -> 48.6 us
  starting transfers between devices: 41.7 us -> 3.65 us
  local copies, waits for them, and re-layouts: 40.5 us -> 5.14 us
  other arithmetic: 34.8 us -> 10.1 us
  blocking collectives: 60.7 us -> 75.5 us
    all_to_all x8 -> x0, waiting for transfers between devices: 304 us -> none  [the longest x4 153 us: to_rows(): lax.all_to_all(values, ('ctx', 'ch'), split_axis=2, concat_axis=4, tiled=...]
    dot_general x16 -> x0, matrix products: 54.3 us -> none  [the longest x2 11.9 us: forward_transform(): jnp.einsum('zsrgmc,mk->zsrgkc', spread, jnp.cos(fine_phase), precision=hi...]
    pallas_call x0 -> x1, Pallas kernels: none -> 48.6 us  [convolutions(): pl.pallas_call(functools.partial(conv_kernel, members, chans, norm), out_...]
    all_to_all x8 -> x0, starting transfers between devices: 37.8 us -> none  [the longest x4 21.4 us: to_columns(): lax.all_to_all(values, ('ctx', 'ch'), split_axis=4, concat_axis=2, tiled=...]
    another operation x7 -> x0, local copies, waits for them, and re-layouts: 17.5 us -> none  [the longest x2 8.33 us: inverse_transform(): jnp.stack([real_part * twist_cos - imag_part * twist_sin, imag_part * twi...]
    psum x1, blocking collectives: 60.7 us -> 75.5 us  [on_device(): short_grad = lax.psum(jnp.stack(short_parts, axis=1), 'ctx')]
    all_to_all x3 -> x0, local copies, waits for them, and re-layouts: 7.27 us -> none  [to_columns(): lax.all_to_all(values, ('ctx', 'ch'), split_axis=4, concat_axis=2, tiled=...]
  transfers between devices with their start and end apart: 10 -> 2, of which waited for: 8 -> 0; matrix products, arithmetic and copies ran while one was open for 12% -> 1% of each run, Pallas kernels for 0% -> 0%
where the time goes in v1:
time: 144 us
  blocking collectives  75.5 us (52%)
  Pallas kernels  48.6 us (34%)
  other arithmetic  10.1 us (7%)
  local copies, waits for them, and re-layouts  5.14 us (4%)
  starting transfers between devices  3.65 us (3%)
    psum x1, blocking collectives, on_device(): short_grad = lax.psum(jnp.stack(short_parts, axis=1), 'ctx')  75.5 us
    pallas_call x1, Pallas kernels, convolutions(): pl.pallas_call(functools.partial(conv_kernel, members, chans, norm), out_...  48.6 us
    add x1, other arithmetic, on_device(): features + short_weight[:, offset, None, :] * extended[:, start:start + b...  4.04 us
    ppermute x2, starting transfers between devices, passed_along(): return lax.ppermute(block, axis, route)  3.65 us
    unnamed x31, local copies, waits for them, and re-layouts  3.17 us
  transfers between devices with their start and end apart: 2, of which 0 were waited for; matrix products, arithmetic and copies ran while one was open for 1% of the time, Pallas kernels for 0%

profile of v1, /device:TPU:0, one launch (start us, length us, event | category | flops | bytes accessed | tf_op | source)
XLA Modules:
  0.0 143.9 jit_solution(9905889028458079825)
XLA Ops:
  0.6 0.7 slice.91
  1.4 2.4 %collective-permute-start = (bf16[3,6,512]{2,1,0:T(8,128)(2,1)S(1)}, bf16[3,6,512]{2,1,0:T(8,128)(2,1)S(1)}, u32[]{:S(2)}, u32[]{:S(2)}) collective-permute-start(bf16[3,6,512]{2,1,0:T(8,128)(2,1)S(1)} %slice.91), channel_id=1, source_target_pairs={{0,2},{2,4},{4,6},{6,8},{8,10},{10,12},{12,14},{14,16},{16,18},{18... | collective-permute-start | bytes 55304 | tf_op jit(solution)/shard_map/ppermute | solution.py:21
  3.7 1.2 fusion.27
  5.0 0.0 collective-permute-done
  5.0 0.0 copy-start.9
  5.0 4.0 %fusion.5 = f32[3,256,512]{2,1,0:T(8,128)S(1)} fusion(bf16[3,256,512]{2,1,0:T(8,128)(2,1)} %param.11, bf16[3,6,512]{2,1,0:T(8,128)(2,1)S(1)} %collective-permute-done, f32[3,512]{1,0:T(4,128)S(1)} %get-tuple-element.31, f32[3,512]{1,0:T(4,128)S(1)} %get-tuple-element.32, f32[3,512]{1,0:T(4,128)S(1)} %get-tuple-element.33, ...), kind=kLoop, calls=%fused_computation.25 | loop fusion | flops 14942208 | bytes 2420736 | tf_op jit(solution)/shard_map/add | solution.py:354
  9.1 0.0 copy-start
  9.1 0.0 copy-start.1
  9.1 0.0 copy-start.2
  9.1 0.0 copy-start.3
  9.1 0.0 copy-start.4
  9.1 0.0 copy-start.5
  9.2 0.0 copy-start.6
  9.2 0.0 copy-start.7
  9.2 0.1 multiply_bitcast_fusion.prod_ref
  9.3 0.1 convert_multiply_fusion.15.grad_ref
  9.4 0.8 copy-done
  10.1 0.2 copy-done.1
  10.3 0.2 copy-done.2
  10.4 0.2 copy-done.3
  10.6 0.2 copy-done.4
  10.8 48.6 %shard_map.138 = f32[3,256,512]{2,1,0:T(8,128)S(1)} custom-call(f32[256,512]{1,0:T(8,128)S(1)} %multiply_bitcast_fusion.prod_ref, f32[256,512]{1,0:T(8,128)S(1)} %copy-done, f32[256,512]{1,0:T(8,128)S(1)} %convert_multiply_fusion.15.grad_ref, f32[9,16]{1,0:T(8,128)S(1)} %copy-done.7, f32[9,16]{1,0:T(8,128)S(1)} %copy-done.6, f32[2,17,256]{2,1,0:T(8,128)S(1)} %copy-done.5, ...), custom_call_target="tpu_custom_call" | custom-call | tf_op jit(solution)/shard_map/pallas_call | solution.py:326
  59.3 0.8 fusion.25
  60.2 1.0 slice_multiply_fusion.6
  61.2 0.1 pad_maximum_fusion.1
  61.4 1.0 copy-done.8
  62.4 1.6 %fusion.11 = (f32[3,512]{1,0:T(4,128)S(1)}, f32[3,512]{1,0:T(4,128)S(1)}, f32[3,512]{1,0:T(4,128)S(1)}, f32[3,512]{1,0:T(4,128)S(1)}, f32[3,512]{1,0:T(4,128)S(1...) fusion(bf16[3,256,512]{2,1,0:T(8,128)(2,1)S(1)} %copy-done.8, bf16[3,6,512]{2,1,0:T(8,128)(2,1)S(1)} %collective-permute-done, ...), kind=kLoop, calls=%fused_computation.31 | loop fusion | flops 16111104 | bytes 2420736 | tf_op jit(solution)/shard_map/reduce_sum | solution.py:376
  64.0 1.3 collective-permute-start.1
  65.3 75.5 %psum.7 = f32[3,7,512]{2,0,1:T(4,128)S(1)} all-reduce(f32[3,7,512]{2,0,1:T(4,128)S(1)} %constant_dynamic-update-slice_fusion), channel_id=1, replica_groups=mesh['ctx'=16,'ch'=2] {'ctx'}, use_global_device_ids=true, to_apply=%region_7.0 | all-reduce | flops 10752 | bytes 86016 | tf_op jit(solution)/shard_map/psum | solution.py:378
  140.9 0.6 copy.15
  141.5 0.2 pad_maximum_fusion
  141.7 2.2 %fusion.14 = bf16[3,256,512]{2,1,0:T(8,128)(2,1)} fusion(f32[3,262,512]{2,1,0:T(8,128)S(1)} %pad_maximum_fusion, f32[3,512]{1,0:T(4,128)S(1)} %get-tuple-element.31, f32[3,512]{1,0:T(4,128)S(1)} %get-tuple-element.32, f32[3,512]{1,0:T(4,128)S(1)} %get-tuple-element.33, f32[3,512]{1,0:T(4,128)S(1)} %get-tuple-element.34, f32[3,512]{1,0:T(4,128)S(1)} %get-tuple-element.35, ...), kind=kLoop, calls=%fused_computation.35 | loop fusion | flops 6291456 | bytes 11839488 | tf_op jit(solution)/shard_map/convert_element_type | solution.py:379
  (19 shorter events, 0.1 us)
Async XLA Ops:
  1.4 3.6 %collective-permute-start = (bf16[3,6,512]{2,1,0:T(8,128)(2,1)S(1)}, bf16[3,6,512]{2,1,0:T(8,128)(2,1)S(1)}, u32[]{:S(2)}, u32[]{:S(2)}) collective-permute-start(bf16[3,6,512]{2,1,0:T(8,128)(2,1)S(1)} %slice.91), channel_id=1, source_target_pairs={{0,2},{2,4},{4,6},{6,8},{8,10},{10,12},{12,14},{14,16},{16,18},{18... | collective-permute-start | bytes 55304 | tf_op jit(solution)/shard_map/ppermute | solution.py:21
  5.0 4.3 %copy-start.9 = (bf16[256,512]{1,0:T(8,128)(2,1)S(1)}, bf16[256,512]{1,0:T(8,128)(2,1)}, u32[]{:S(2)}) copy-start(bf16[256,512]{1,0:T(8,128)(2,1)} %param.14) | copy-start | bytes 786436
  9.1 1.0 copy-start
  9.1 1.2 copy-start.1
  9.1 1.3 copy-start.2
  9.1 1.5 %copy-start.3 = (bf16[512,512]{1,0:T(8,128)(2,1)S(1)}, bf16[512,512]{1,0:T(8,128)(2,1)}, u32[]{:S(2)}) copy-start(bf16[512,512]{1,0:T(8,128)(2,1)} %constant.20.clone.fwd_low) | copy-start | bytes 1572868
  9.1 1.6 %copy-start.4 = (bf16[512,512]{1,0:T(8,128)(2,1)S(1)}, bf16[512,512]{1,0:T(8,128)(2,1)}, u32[]{:S(2)}) copy-start(bf16[512,512]{1,0:T(8,128)(2,1)} %constant.19.clone.fwd_high) | copy-start | bytes 1572868
  9.1 1.6 %copy-start.5 = (f32[2,17,256]{2,1,0:T(8,128)S(1)}, f32[2,17,256]{2,1,0:T(8,128)}, u32[]{:S(2)}) copy-start(f32[2,17,256]{2,1,0:T(8,128)} %constant.18.clone.twist_ref) | copy-start | bytes 104452
  9.2 1.6 %copy-start.6 = (f32[9,16]{1,0:T(8,128)S(1)}, f32[9,16]{1,0:T(8,128)}, u32[]{:S(2)}) copy-start(f32[9,16]{1,0:T(8,128)} %constant.17.clone.sin_ref) | copy-start | bytes 1732
  9.2 1.6 %copy-start.7 = (f32[9,16]{1,0:T(8,128)S(1)}, f32[9,16]{1,0:T(8,128)}, u32[]{:S(2)}) copy-start(f32[9,16]{1,0:T(8,128)} %constant.16.clone.cos_ref) | copy-start | bytes 1732
  61.2 1.1 copy-start.8
  64.0 77.6 %collective-permute-start.1 = (bf16[3,6,512]{2,1,0:T(8,128)(2,1)S(1)}, bf16[3,6,512]{2,1,0:T(8,128)(2,1)S(1)}, u32[]{:S(2)}, u32[]{:S(2)}) collective-permute-start(bf16[3,6,512]{2,1,0:T(8,128)(2,1)S(1)} %slice.233), channel_id=1, source_target_pairs={{2,0},{4,2},{6,4},{8,6},{10,8},{12,10},{14,12},{16,14},{18,16},{20... | collective-permute-start | bytes 55304 | tf_op jit(solution)/shard_map/ppermute | solution.py:21

commit v2 on v0

v2 whole, which is shorter than its diff:
```python
import functools
import math

import jax
import jax.numpy as jnp
import numpy as np
from jax import lax
from jax.experimental import pallas as pl
from jax.experimental.pallas import tpu as pltpu
from jax.sharding import PartitionSpec as P

span = 250.0
half_span = 125.0
tiny = 1e-30
edge = 8
step_rows = 32
f32 = jnp.float32


def encode(values, top):
    power = jnp.abs(values) * (span / top) - half_span
    code = jnp.exp2(power)
    return jnp.where(values < 0.0, -code, code).astype(jnp.bfloat16)


def decode(code, top):
    code = code.astype(f32)
    size = (jnp.log2(jnp.abs(code)) + half_span) * (top * (1.0 / span))
    return jnp.where(code < 0.0, -size, size)


def row_top(values):
    return jnp.maximum(jnp.max(jnp.abs(values), axis=1, keepdims=True), tiny)


def to_lanes(column):
    rows = column.shape[0]
    lane = lax.broadcasted_iota(jnp.int32, (rows, 128), 1)
    row = lax.broadcasted_iota(jnp.int32, (rows, 128), 0)
    return jnp.sum(jnp.where(lane == row, column, 0.0), axis=0, keepdims=True)


def to_column(line, rows):
    lane = lax.broadcasted_iota(jnp.int32, (rows, 128), 1)
    row = lax.broadcasted_iota(jnp.int32, (rows, 128), 0)
    return jnp.sum(jnp.where(lane == row, line, 0.0), axis=1, keepdims=True)


def three_products(values, high_ref, low_ref):
    high = values.astype(jnp.bfloat16)
    low = (values - high.astype(f32)).astype(jnp.bfloat16)
    dot = functools.partial(jnp.dot, preferred_element_type=f32)
    return dot(high, high_ref[...]) + (dot(low, high_ref[...]) + dot(high, low_ref[...]))


def feature_rows(extended_ref, weight_ref, which, start):
    taps = weight_ref.shape[1]
    window = extended_ref[which, pl.ds(start, step_rows + edge), :]
    total = weight_ref[which, 0:1, :] * window[edge : edge + step_rows]
    for tap in range(1, taps):
        total = total + weight_ref[which, tap : tap + 1, :] * window[edge - tap : edge - tap + step_rows]
    return total


def hyena_kernel(
    members, norm, streams_ref, weight_ref, filt_ref, cot_ref, cos_ref, sin_ref, twist_ref,
    fwd_high, fwd_low, inv_high, inv_low,
    hyena_ref, stream_grad_ref, short_ref, filter_grad_ref,
    turned, packed, tops, got, got_tops, back, back_tops, last_tops, home, home_tops, home_last,
    waves, spectra, work, features, extended, grads, halo, edge_out, edge_in, parts, gathered, sums,
    send_sem, recv_sem, top_send, top_recv, back_send, back_recv, back_top_send, back_top_recv,
    last_send, last_recv, halo_sem, edge_sem, part_send, part_recv, sum_send, sum_recv,
):
    me = lax.axis_index("ctx")
    mine = lax.axis_index("ch")
    rows, width = filt_ref.shape
    chans = width // members
    half = members // 2
    taps = weight_ref.shape[1]
    lane_tiles = width // 128
    pieces = 3 * lane_tiles
    chunks = rows // step_rows

    def remote(source, target, sent, received, other):
        return pltpu.make_async_remote_copy(
            src_ref=source, dst_ref=target, send_sem=sent, recv_sem=received,
            device_id=(other, mine), device_id_type=pl.DeviceIdType.MESH,
        )

    def others(body):
        def one(step, carry):
            body(lax.rem(me + step, members))
            return carry

        lax.fori_loop(1, members, one, 0)

    def outward(which, other, source):
        return remote(
            packed.at[which, other], got.at[which, source],
            send_sem.at[which], recv_sem.at[which], other,
        )

    def outward_top(other, source):
        return remote(
            tops.at[other], got_tops.at[source], top_send.at[0], top_recv.at[0], other
        )

    def homeward(which, other, source):
        return remote(
            back.at[which, other], home.at[which, source],
            back_send.at[which], back_recv.at[which], other,
        )

    def homeward_top(other, source):
        return remote(
            back_tops.at[other], home_tops.at[source],
            back_top_send.at[0], back_top_recv.at[0], other,
        )

    def homeward_last(other, source):
        return remote(
            last_tops.at[other], home_last.at[source],
            last_send.at[0], last_recv.at[0], other,
        )

    def part_out(piece, source):
        return remote(
            parts.at[piece], gathered.at[source], part_send.at[piece], part_recv.at[0], piece
        )

    def sum_out(other, piece):
        return remote(
            sums.at[piece], sums.at[piece], sum_send.at[0], sum_recv.at[piece], other
        )

    most = pl.ds(0, members - 1)
    near = lax.rem(me + 1, members)

    def outward_all(which):
        return remote(
            packed.at[which, most], got.at[which, most], send_sem.at[which], recv_sem.at[which], near
        )

    def homeward_all(which):
        return remote(
            back.at[which, most], home.at[which, most], back_send.at[which], back_recv.at[which], near
        )

    outward_top_all = remote(
        tops.at[most], got_tops.at[most], top_send.at[0], top_recv.at[0], near
    )
    homeward_top_all = remote(
        back_tops.at[most], home_tops.at[most], back_top_send.at[0], back_top_recv.at[0], near
    )
    homeward_last_all = remote(
        last_tops.at[most], home_last.at[most], last_send.at[0], last_recv.at[0], near
    )
    part_all = remote(
        gathered.at[most], gathered.at[most], sum_send.at[0], part_recv.at[0], near
    )
    sum_all = remote(
        gathered.at[most], gathered.at[most], sum_send.at[0], part_recv.at[0], near
    )

    barrier = pltpu.get_barrier_semaphore()

    def greet(other):
        pl.semaphore_signal(
            barrier, inc=1, device_id=(other, mine), device_id_type=pl.DeviceIdType.MESH
        )

    others(greet)

    def pack(which, other):
        values = turned[which, other * chans : other * chans + chans, :]
        top = row_top(values)
        packed[which, other] = encode(values, top)
        tops[other, :, which * 128 : which * 128 + 128] = to_lanes(top)

    def pack_all(which):
        for other in range(members):
            pack(which, other)

    halo_out = remote(
        streams_ref.at[:, pl.ds(rows - 16, 16), :], halo, halo_sem.at[0], halo_sem.at[1],
        lax.rem(me + 1, members),
    )
    turned[0] = filt_ref[...].T
    pack_all(0)
    pl.semaphore_wait(barrier, members - 1)

    @pl.when(me < members - 1)
    def _():
        halo_out.start()

    others(lambda other: outward(0, other, me).start())
    got[0, me] = packed[0, me]

    for which in range(3):
        extended[which, edge:, :] = streams_ref[which].astype(f32)

    @pl.when(me > 0)
    def _():
        halo_out.wait_recv()
        for which in range(3):
            extended[which, :edge, :] = halo[which].astype(f32)[16 - edge :]

    @pl.when(me == 0)
    def _():
        extended[:, :edge, :] = jnp.zeros((3, edge, width), f32)

    def featurize(step, carry):
        start = pl.multiple_of(step * step_rows, step_rows)
        query, key, value = [
            feature_rows(extended, weight_ref, which, start) for which in range(3)
        ]
        here = pl.ds(start, step_rows)
        features[0, here, :] = query
        features[1, here, :] = key
        features[2, here, :] = value
        grads[0, here, :] = key * value
        grads[1, here, :] = cot_ref[here, :].astype(f32) * query
        return carry

    lax.fori_loop(0, chunks, featurize, 0)
    turned[1] = grads[0, :rows, :].T
    turned[2] = grads[1, :rows, :].T
    pack_all(1)
    pack_all(2)
    others(lambda other: outward_top(other, me).start())
    others(lambda other: outward(1, other, me).start())
    others(lambda other: outward(2, other, me).start())
    got[1, me] = packed[1, me]
    got[2, me] = packed[2, me]
    got_tops[me] = tops[me]
    outward_top_all.wait_recv()

    height = (members + 1) * chans

    def forward(which):
        outward_all(which).wait_recv()
        for source in range(members):
            top = to_column(got_tops[source, :, which * 128 : which * 128 + 128], chans)
            if which == 0:
                top = top * norm
            waves[source] = decode(got[which, source], top)

        def coarse(freq, carry):
            sides = []
            for parity in range(2):
                real = jnp.zeros((chans, rows), f32)
                imag = jnp.zeros((chans, rows), f32)
                for block in range(parity, members, 2):
                    value = waves[block]
                    real = real + cos_ref[freq, block] * value
                    imag = imag - sin_ref[freq, block] * value
                sides.append((real, imag))
            (even_r, even_i), (odd_r, odd_i) = sides

            def put(place, real, imag):
                cosine = twist_ref[0, pl.ds(place, 1), :]
                sine = twist_ref[1, pl.ds(place, 1), :]
                spectra[which, place, :, :rows] = real * cosine + imag * sine
                spectra[which, place, :, rows:] = imag * cosine - real * sine

            put(members - freq, even_r - odd_r, odd_i - even_i)
            put(freq, even_r + odd_r, even_i + odd_i)
            return carry

        lax.fori_loop(0, half + 1, coarse, 0)
        flat = spectra[which].reshape(height, 2 * rows)
        spectra[which] = three_products(flat, fwd_high, fwd_low).reshape(
            members + 1, chans, 2 * rows
        )

    def inverse(which, left, right, sign):
        def multiply(freq, carry):
            lr, li = spectra[left, freq, :, :rows], spectra[left, freq, :, rows:] * sign
            rr, ri = spectra[right, freq, :, :rows], spectra[right, freq, :, rows:]
            work[freq, :, :rows] = lr * rr - li * ri
            work[freq, :, rows:] = lr * ri + li * rr
            return carry

        lax.fori_loop(0, members + 1, multiply, 0)
        flat = work[...].reshape(height, 2 * rows)
        work[...] = three_products(flat, inv_high, inv_low).reshape(members + 1, chans, 2 * rows)

        def untwist(freq, carry):
            def turn(place):
                cosine = twist_ref[0, pl.ds(place, 1), :]
                sine = twist_ref[1, pl.ds(place, 1), :]
                real = work[place, :, :rows]
                imag = work[place, :, rows:]
                return real * cosine - imag * sine, imag * cosine + real * sine

            lr, li = turn(freq)
            ur, ui = turn(members - freq)
            ones = jnp.where(freq == half, 0.0, 1.0)
            weight = jnp.where(freq == 0, 1.0, 2.0) * (scale / (2.0 * members * rows))
            work[freq, :, :rows] = weight * (lr + ones * ur)
            work[freq, :, rows:] = weight * (li - ones * ui)

            @pl.when(freq < half)
            def _():
                work[members - freq, :, :rows] = weight * (lr - ur)
                work[members - freq, :, rows:] = weight * (li + ui)

            return carry

        scale = norm if which == 2 else 1.0
        lax.fori_loop(0, half + 1, untwist, 0)

        def total_of(block, odd):
            total = jnp.zeros((chans, rows), f32)
            for freq in range(half + 1):
                place = members - freq if odd else freq
                total = total + cos_ref[freq, block] * work[place, :, :rows]
                total = total - sin_ref[freq, block] * work[place, :, rows:]
            return total

        def finish(step, carry):
            blocks = [step * 4 + place for place in range(4)]
            totals = [total_of(block, place % 2 == 1) for place, block in enumerate(blocks)]
            for block, total in zip(blocks, totals):
                top = row_top(total)
                back[which, block] = encode(total, top)
                if which < 2:
                    back_tops[block, :, which * 128 : which * 128 + 128] = to_lanes(top)
                else:
                    last_tops[block] = to_lanes(top)
            for block in blocks:

                @pl.when(block != me)
                def _():
                    homeward(which, block, me).start()
                    if which == 1:
                        homeward_top(block, me).start()
                    if which == 2:
                        homeward_last(block, me).start()

            return carry

        lax.fori_loop(0, members // 4, finish, 0)
        home[which, me] = back[which, me]
        if which == 1:
            home_tops[me] = back_tops[me]
        if which == 2:
            home_last[me] = last_tops[me]

    forward(0)
    forward(1)
    inverse(0, 0, 1, 1.0)
    forward(2)
    inverse(1, 0, 2, -1.0)
    inverse(2, 1, 2, -1.0)

    def settle(which):
        homeward_all(which).wait_recv()
        if which == 2:
            homeward_last_all.wait_recv()
        for source in range(members):
            if which < 2:
                line = home_tops[source, :, which * 128 : which * 128 + 128]
            else:
                line = home_last[source]
            turned[which, source * chans : source * chans + chans, :] = decode(
                home[which, source], to_column(line, chans)
            )

    homeward_top_all.wait_recv()
    settle(0)
    settle(1)
    grads[0, :rows, :] = turned[0].T
    grads[1, :rows, :] = turned[1].T

    def gate(step, carry):
        start = pl.multiple_of(step * step_rows, step_rows)
        here = pl.ds(start, step_rows)
        mixed = grads[0, here, :]
        grad_product = grads[1, here, :]
        hyena_ref[here, :] = (features[0, here, :] * mixed).astype(jnp.bfloat16)
        grads[0, here, :] = cot_ref[here, :].astype(f32) * mixed
        grads[1, here, :] = grad_product * features[2, here, :]
        grads[2, here, :] = grad_product * features[1, here, :]
        return carry

    gate(0, 0)
    edge_out[...] = grads[:, :edge, :]
    edge_copy = remote(
        edge_out, edge_in, edge_sem.at[0], edge_sem.at[1], lax.rem(me + members - 1, members)
    )

    @pl.when(me > 0)
    def _():
        edge_copy.start()

    lax.fori_loop(1, chunks, gate, 0)

    for which in range(3):

        def tap_sums(step, carry):
            start = pl.multiple_of(step * step_rows, step_rows)
            window = extended[which, pl.ds(start, step_rows + edge), :]
            grad = grads[which, pl.ds(start, step_rows), :]
            return tuple(
                total
                + jnp.sum(
                    (grad * window[edge - tap : edge - tap + step_rows]).reshape(
                        step_rows // 8, 8, width
                    ),
                    axis=0,
                )
                for tap, total in enumerate(carry)
            )

        totals = lax.fori_loop(
            0, chunks, tap_sums, tuple(jnp.zeros((8, width), f32) for _ in range(taps))
        )
        lines = [jnp.sum(total, axis=0, keepdims=True) for total in totals]
        lines.append(jnp.zeros((8 - taps, width), f32))
        block = jnp.concatenate(lines, axis=0)
        for tile in range(lane_tiles):
            parts[which * lane_tiles + tile] = block[:, tile * 128 : tile * 128 + 128]

    def each_piece(body):
        def one(piece, carry):
            @pl.when(piece != me)
            def _():
                body(piece)

            return carry

        lax.fori_loop(0, pieces, one, 0)

    each_piece(lambda piece: part_out(piece, me).start())

    @pl.when(me < members - 1)
    def _():
        edge_copy.wait_recv()
        grads[:, rows:, :] = edge_in[...]

    @pl.when(me == members - 1)
    def _():
        grads[:, rows:, :] = jnp.zeros((3, edge, width), f32)

    def back_taps(step, carry):
        start = pl.multiple_of(step * step_rows, step_rows)
        for which in range(3):
            window = grads[which, pl.ds(start, step_rows + edge), :]
            total = weight_ref[which, 0:1, :] * window[:step_rows]
            for tap in range(1, taps):
                total = total + weight_ref[which, tap : tap + 1, :] * window[tap : tap + step_rows]
            stream_grad_ref[which, pl.ds(start, step_rows), :] = total.astype(jnp.bfloat16)
        return carry

    lax.fori_loop(0, chunks, back_taps, 0)

    @pl.when(me < pieces)
    def _():
        gathered[me] = parts[me]
        part_all.wait_recv()
        total = gathered[0]
        for source in range(1, members):
            total = total + gathered[source]
        sums[me] = total
        others(lambda other: sum_out(other, me).start())

    settle(2)
    filter_grad_ref[...] = turned[2].T

    each_piece(lambda piece: sum_out(piece, piece).wait_recv())
    for which in range(3):
        for tile in range(lane_tiles):
            short_ref[which, :, tile * 128 : tile * 128 + 128] = sums[which * lane_tiles + tile][
                :taps
            ]

    for which in range(3):
        outward_all(which).wait_send()
        homeward_all(which).wait_send()
    outward_top_all.wait_send()
    homeward_top_all.wait_send()
    homeward_last_all.wait_send()
    each_piece(lambda piece: part_out(piece, me).wait_send())

    @pl.when(me < pieces)
    def _():
        sum_all.wait_send()

    @pl.when(me < members - 1)
    def _():
        halo_out.wait_send()

    @pl.when(me > 0)
    def _():
        edge_copy.wait_send()


def tables(members, rows):
    period = 2 * members * rows
    coarse = np.outer(np.arange(members // 2 + 1), np.arange(members)) % (2 * members)
    coarse = coarse * (math.pi / members)
    twist = np.outer(np.arange(members + 1), np.arange(rows)) % period * (2.0 * math.pi / period)
    fine = np.outer(np.arange(rows), np.arange(rows)) % rows * (2.0 * math.pi / rows)
    c, s = np.cos(fine), np.sin(fine)
    forward = np.block([[c, -s], [s, c]])

    def split(matrix):
        high = matrix.astype(jnp.bfloat16)
        return high, (matrix - high.astype(np.float64)).astype(jnp.bfloat16)

    return (
        np.cos(coarse).astype(np.float32),
        np.sin(coarse).astype(np.float32),
        np.stack([np.cos(twist), np.sin(twist)]).astype(np.float32),
        *split(forward),
        *split(forward.T),
    )


def hand_over(*refs):
    sem = refs[8]
    copies = [
        pltpu.make_async_copy(source, target, sem.at[place])
        for place, (source, target) in enumerate(zip(refs[:4], refs[4:8]))
    ]
    for copy in copies:
        copy.start()
    for copy in copies:
        copy.wait()


def on_device(streams, short_weight, long_filter, cotangent):
    members = lax.axis_size("ctx")
    rows, width = long_filter.shape
    chans = width // members
    pieces = 3 * (width // 128)
    norm = 1.0 / math.sqrt(rows * members)
    vmem = pl.BlockSpec(memory_space=pltpu.VMEM)
    smem = pl.BlockSpec(memory_space=pltpu.SMEM)
    wire = pltpu.VMEM((3, members, chans, rows), jnp.bfloat16)
    dma = pltpu.SemaphoreType.DMA
    results = tuple(
        pl.pallas_call(
            functools.partial(hyena_kernel, members, norm),
            out_shape=(
                jax.ShapeDtypeStruct((rows, width), jnp.bfloat16),
                jax.ShapeDtypeStruct(streams.shape, jnp.bfloat16),
                jax.ShapeDtypeStruct(short_weight.shape, f32),
                jax.ShapeDtypeStruct((rows, width), f32),
            ),
            in_specs=[vmem] * 4 + [smem] * 2 + [vmem] * 5,
            out_specs=(vmem,) * 4,
            scratch_shapes=[
                pltpu.VMEM((3, width, rows), f32),
                wire,
                pltpu.VMEM((members, 1, 384), f32),
                wire,
                pltpu.VMEM((members, 1, 384), f32),
                wire,
                pltpu.VMEM((members, 1, 256), f32),
                pltpu.VMEM((members, 1, 128), f32),
                wire,
                pltpu.VMEM((members, 1, 256), f32),
                pltpu.VMEM((members, 1, 128), f32),
                pltpu.VMEM((members, chans, rows), f32),
                pltpu.VMEM((3, members + 1, chans, 2 * rows), f32),
                pltpu.VMEM((members + 1, chans, 2 * rows), f32),
                pltpu.VMEM((3, rows, width), f32),
                pltpu.VMEM((3, rows + edge, width), f32),
                pltpu.VMEM((3, rows + edge, width), f32),
                pltpu.VMEM((3, 16, width), jnp.bfloat16),
                pltpu.VMEM((3, edge, width), f32),
                pltpu.VMEM((3, edge, width), f32),
                pltpu.VMEM((pieces, 8, 128), f32),
                pltpu.VMEM((members, 8, 128), f32),
                pltpu.VMEM((pieces, 8, 128), f32),
                dma((3,)),
                dma((3,)),
                dma((1,)),
                dma((1,)),
                dma((3,)),
                dma((3,)),
                dma((1,)),
                dma((1,)),
                dma((1,)),
                dma((1,)),
                dma((2,)),
                dma((2,)),
                dma((pieces,)),
                dma((1,)),
                dma((1,)),
                dma((pieces,)),
            ],
            compiler_params=pltpu.CompilerParams(
                collective_id=0, has_side_effects=True, vmem_limit_bytes=56 * 1024 * 1024
            ),
        )(
            streams, short_weight, long_filter, cotangent,
            *[jnp.asarray(t) for t in tables(members, rows)],
        )
    )
    anywhere = pl.BlockSpec(memory_space=pl.ANY)
    return tuple(
        pl.pallas_call(
            hand_over,
            out_shape=tuple(jax.ShapeDtypeStruct(r.shape, r.dtype) for r in results),
            in_specs=[anywhere] * 4,
            out_specs=(anywhere,) * 4,
            scratch_shapes=[dma((4,))],
            compiler_params=pltpu.CompilerParams(vmem_limit_bytes=60 * 1024 * 1024),
        )(*results)
    )


def solution(mesh):
    placed = (P(None, "ctx", "ch"), P(None, None, "ch"), P("ctx", "ch"), P("ctx", "ch"))
    return jax.shard_map(
        on_device,
        mesh=mesh,
        in_specs=placed,
        out_specs=(P("ctx", "ch"), P(None, "ctx", "ch"), P(None, None, "ch"), P("ctx", "ch")),
        check_vma=False,
    )
```

time: 547 us -> 108 us (0.20); the launches traced: 538 us -> 108 us
  waiting for transfers between devices: 304 us -> 0 us
  Pallas kernels: 0 us -> 107 us
  blocking collectives: 60.7 us -> 0 us
  matrix products: 54.3 us -> 0 us
  starting transfers between devices: 41.7 us -> 0 us
  local copies, waits for them, and re-layouts: 40.5 us -> 0 us
  other arithmetic: 34.8 us -> 0 us
    all_to_all x8 -> x0, waiting for transfers between devices: 304 us -> none  [the longest x4 153 us: to_rows(): lax.all_to_all(values, ('ctx', 'ch'), split_axis=2, concat_axis=4, tiled=...]
    pallas_call x0 -> x2, Pallas kernels: none -> 107 us  [the longest x1 57.1 us: on_device(): pl.pallas_call(functools.partial(hyena_kernel, members, norm), out_shape=...]
    psum x1 -> x0, blocking collectives: 60.7 us -> none  [on_device(): short_grad = lax.psum(jnp.stack(short_parts, axis=1), 'ctx')]
    dot_general x16 -> x0, matrix products: 54.3 us -> none  [the longest x2 11.9 us: forward_transform(): jnp.einsum('zsrgmc,mk->zsrgkc', spread, jnp.cos(fine_phase), precision=hi...]
    all_to_all x8 -> x0, starting transfers between devices: 37.8 us -> none  [the longest x4 21.4 us: to_columns(): lax.all_to_all(values, ('ctx', 'ch'), split_axis=4, concat_axis=2, tiled=...]
    another operation x8 -> x0, local copies, waits for them, and re-layouts: 17.5 us -> none  [the longest x2 8.33 us: inverse_transform(): jnp.stack([real_part * twist_cos - imag_part * twist_sin, imag_part * twi...]
    add x4 -> x0, other arithmetic: 8.34 us -> none  [the longest x1 5.55 us: on_device(): features + short_weight[:, offset, None, :] * extended[:, start:start + b...]
    all_to_all x3 -> x0, local copies, waits for them, and re-layouts: 7.27 us -> none  [to_columns(): lax.all_to_all(values, ('ctx', 'ch'), split_axis=4, concat_axis=2, tiled=...]
  transfers between devices with their start and end apart: 10 -> 0, of which waited for: 8 -> 0; matrix products, arithmetic and copies ran while one was open for 12% -> 0% of each run, Pallas kernels for 0% -> 0%
where the time goes in v2:
time: 108 us
  Pallas kernels  107 us (99%)
    pallas_call x1, Pallas kernels, on_device(): pl.pallas_call(functools.partial(hyena_kernel, members, norm), out_shape=...  57.1 us
    pallas_call x1, Pallas kernels, on_device(): pl.pallas_call(hand_over, out_shape=tuple((jax.ShapeDtypeStruct(r.shape,...  50.3 us

profile of v2, /device:TPU:0, one launch (start us, length us, event | category | flops | bytes accessed | tf_op | source)
XLA Modules:
  0.0 108.0 jit_solution(15519437260516528379)
XLA Ops:
  0.6 57.1 %shard_map.138 = (bf16[256,512]{1,0:T(8,128)(2,1)}, bf16[3,256,512]{2,1,0:T(8,128)(2,1)}, f32[3,7,512]{2,1,0:T(8,128)}, f32[256,512]{1,0:T(8,128)}) custom-call(bf16[3,256,512]{2,1,0:T(8,128)(2,1)} %streams_ref.1, f32[3,7,512]{2,1,0:T(8,128)} %weight_ref.1, f32[256,512]{1,0:T(8,128)} %filt_ref.1, bf16[256,512]{1,0:T(8,128)(2,1)} %cot_ref.1, ...), custom_call_target="tpu_custom_call" | custom-call | tf_op jit(solution)/shard_map/pallas_call | solution.py:544
  57.7 50.3 %shard_map.139 = (bf16[256,512]{1,0:T(8,128)(2,1)}, bf16[3,256,512]{2,1,0:T(8,128)(2,1)}, f32[3,7,512]{2,1,0:T(8,128)}, f32[256,512]{1,0:T(8,128)}) custom-call(bf16[256,512]{1,0:T(8,128)(2,1)} %get-tuple-element.8.refs_0_, bf16[3,256,512]{2,1,0:T(8,128)(2,1)} %get-tuple-element.9.refs_1_, f32[3,7,512]{2,1,0:T(8,128)} %get-tuple-element.10.refs_2_, ...), custom_call_target="tpu_custom_call" | custom-call | tf_op jit(solution)/shard_map/pallas_call | solution.py:605

commit v3 on v2

--- a/solution.py
+++ b/solution.py
@@ -46,11 +46,12 @@
     return jnp.sum(jnp.where(lane == row, line, 0.0), axis=1, keepdims=True)
 
 
-def three_products(values, high_ref, low_ref):
+def three_products(values, table_ref):
     high = values.astype(jnp.bfloat16)
     low = (values - high.astype(f32)).astype(jnp.bfloat16)
-    dot = functools.partial(jnp.dot, preferred_element_type=f32)
-    return dot(high, high_ref[...]) + (dot(low, high_ref[...]) + dot(high, low_ref[...]))
+    return jnp.dot(
+        jnp.concatenate([high, low, high], axis=1), table_ref[...], preferred_element_type=f32
+    )
 
 
 def feature_rows(extended_ref, weight_ref, which, start):
@@ -64,12 +65,13 @@
 
 def hyena_kernel(
     members, norm, streams_ref, weight_ref, filt_ref, cot_ref, cos_ref, sin_ref, twist_ref,
-    fwd_high, fwd_low, inv_high, inv_low,
+    fwd_any, inv_any,
     hyena_ref, stream_grad_ref, short_ref, filter_grad_ref,
-    turned, packed, tops, got, got_tops, back, back_tops, last_tops, home, home_tops, home_last,
+    turned, packed, tops, got, got_tops, back, back_tops, home, home_tops,
     waves, spectra, work, features, extended, grads, halo, edge_out, edge_in, parts, gathered, sums,
     send_sem, recv_sem, top_send, top_recv, back_send, back_recv, back_top_send, back_top_recv,
-    last_send, last_recv, halo_sem, edge_sem, part_send, part_recv, sum_send, sum_recv,
+    halo_sem, edge_sem, part_send, part_recv, sum_send, sum_recv,
+    fwd_ref, inv_ref, table_sem,
 ):
     me = lax.axis_index("ctx")
     mine = lax.axis_index("ch")
@@ -111,16 +113,10 @@
             back_send.at[which], back_recv.at[which], other,
         )
 
-    def homeward_top(other, source):
-        return remote(
-            back_tops.at[other], home_tops.at[source],
-            back_top_send.at[0], back_top_recv.at[0], other,
-        )
-
-    def homeward_last(other, source):
-        return remote(
-            last_tops.at[other], home_last.at[source],
-            last_send.at[0], last_recv.at[0], other,
+    def homeward_top(which, other, source):
+        return remote(
+            back_tops.at[which, other], home_tops.at[which, source],
+            back_top_send.at[which], back_top_recv.at[which], other,
         )
 
     def part_out(piece, source):
@@ -149,12 +145,12 @@
     outward_top_all = remote(
         tops.at[most], got_tops.at[most], top_send.at[0], top_recv.at[0], near
     )
-    homeward_top_all = remote(
-        back_tops.at[most], home_tops.at[most], back_top_send.at[0], back_top_recv.at[0], near
-    )
-    homeward_last_all = remote(
-        last_tops.at[most], home_last.at[most], last_send.at[0], last_recv.at[0], near
-    )
+    def homeward_top_all(which):
+        return remote(
+            back_tops.at[which, most], home_tops.at[which, most],
+            back_top_send.at[which], back_top_recv.at[which], near,
+        )
+
     part_all = remote(
         gathered.at[most], gathered.at[most], sum_send.at[0], part_recv.at[0], near
     )
@@ -170,6 +166,10 @@
         )
 
     others(greet)
+    fwd_copy = pltpu.make_async_copy(fwd_any, fwd_ref, table_sem.at[0])
+    inv_copy = pltpu.make_async_copy(inv_any, inv_ref, table_sem.at[1])
+    fwd_copy.start()
+    inv_copy.start()
 
     def pack(which, other):
         values = turned[which, other * chans : other * chans + chans, :]
@@ -269,7 +269,7 @@
 
         lax.fori_loop(0, half + 1, coarse, 0)
         flat = spectra[which].reshape(height, 2 * rows)
-        spectra[which] = three_products(flat, fwd_high, fwd_low).reshape(
+        spectra[which] = three_products(flat, fwd_ref).reshape(
             members + 1, chans, 2 * rows
         )
 
@@ -283,7 +283,7 @@
 
         lax.fori_loop(0, members + 1, multiply, 0)
         flat = work[...].reshape(height, 2 * rows)
-        work[...] = three_products(flat, inv_high, inv_low).reshape(members + 1, chans, 2 * rows)
+        work[...] = three_products(flat, inv_ref).reshape(members + 1, chans, 2 * rows)
 
         def untwist(freq, carry):
             def turn(place):
@@ -324,80 +324,60 @@
             for block, total in zip(blocks, totals):
                 top = row_top(total)
                 back[which, block] = encode(total, top)
-                if which < 2:
-                    back_tops[block, :, which * 128 : which * 128 + 128] = to_lanes(top)
-                else:
-                    last_tops[block] = to_lanes(top)
+                back_tops[which, block] = to_lanes(top)
             for block in blocks:
 
                 @pl.when(block != me)
                 def _():
                     homeward(which, block, me).start()
-                    if which == 1:
-                        homeward_top(block, me).start()
-                    if which == 2:
-                        homeward_last(block, me).start()
+                    homeward_top(which, block, me).start()
 
             return carry
 
         lax.fori_loop(0, members // 4, finish, 0)
         home[which, me] = back[which, me]
-        if which == 1:
-            home_tops[me] = back_tops[me]
-        if which == 2:
-            home_last[me] = last_tops[me]
-
+        home_tops[which, me] = back_tops[which, me]
+
+    fwd_copy.wait()
     forward(0)
     forward(1)
+    inv_copy.wait()
     inverse(0, 0, 1, 1.0)
     forward(2)
     inverse(1, 0, 2, -1.0)
     inverse(2, 1, 2, -1.0)
 
     def settle(which):
+        homeward_top_all(which).wait_recv()
         homeward_all(which).wait_recv()
-        if which == 2:
-            homeward_last_all.wait_recv()
         for source in range(members):
-            if which < 2:
-                line = home_tops[source, :, which * 128 : which * 128 + 128]
-            else:
-                line = home_last[source]
             turned[which, source * chans : source * chans + chans, :] = decode(
-                home[which, source], to_column(line, chans)
+                home[which, source], to_column(home_tops[which, source], chans)
             )
 
-    homeward_top_all.wait_recv()
-    settle(0)
-    settle(1)
-    grads[0, :rows, :] = turned[0].T
-    grads[1, :rows, :] = turned[1].T
-
-    def gate(step, carry):
-        start = pl.multiple_of(step * step_rows, step_rows)
-        here = pl.ds(start, step_rows)
+    before = lax.rem(me + members - 1, members)
+    query_edge = remote(
+        edge_out.at[0], edge_in.at[0], edge_sem.at[0], edge_sem.at[1], before
+    )
+    other_edges = remote(
+        edge_out.at[pl.ds(1, 2)], edge_in.at[pl.ds(1, 2)], edge_sem.at[2], edge_sem.at[3], before
+    )
+
+    def gate_query(step, carry):
+        here = pl.ds(pl.multiple_of(step * step_rows, step_rows), step_rows)
         mixed = grads[0, here, :]
-        grad_product = grads[1, here, :]
         hyena_ref[here, :] = (features[0, here, :] * mixed).astype(jnp.bfloat16)
         grads[0, here, :] = cot_ref[here, :].astype(f32) * mixed
+        return carry
+
+    def gate_others(step, carry):
+        here = pl.ds(pl.multiple_of(step * step_rows, step_rows), step_rows)
+        grad_product = grads[1, here, :]
         grads[1, here, :] = grad_product * features[2, here, :]
         grads[2, here, :] = grad_product * features[1, here, :]
         return carry
 
-    gate(0, 0)
-    edge_out[...] = grads[:, :edge, :]
-    edge_copy = remote(
-        edge_out, edge_in, edge_sem.at[0], edge_sem.at[1], lax.rem(me + members - 1, members)
-    )
-
-    @pl.when(me > 0)
-    def _():
-        edge_copy.start()
-
-    lax.fori_loop(1, chunks, gate, 0)
-
-    for which in range(3):
-
+    def all_taps(which):
         def tap_sums(step, carry):
             start = pl.multiple_of(step * step_rows, step_rows)
             window = extended[which, pl.ds(start, step_rows + edge), :]
@@ -422,6 +402,28 @@
         for tile in range(lane_tiles):
             parts[which * lane_tiles + tile] = block[:, tile * 128 : tile * 128 + 128]
 
+    settle(0)
+    grads[0, :rows, :] = turned[0].T
+    lax.fori_loop(0, chunks, gate_query, 0)
+    edge_out[0] = grads[0, :edge, :]
+
+    @pl.when(me > 0)
+    def _():
+        query_edge.start()
+
+    all_taps(0)
+    settle(1)
+    grads[1, :rows, :] = turned[1].T
+    lax.fori_loop(0, chunks, gate_others, 0)
+    edge_out[1:] = grads[1:, :edge, :]
+
+    @pl.when(me > 0)
+    def _():
+        other_edges.start()
+
+    all_taps(1)
+    all_taps(2)
+
     def each_piece(body):
         def one(piece, carry):
             @pl.when(piece != me)
@@ -436,7 +438,8 @@
 
     @pl.when(me < members - 1)
     def _():
-        edge_copy.wait_recv()
+        query_edge.wait_recv()
+        other_edges.wait_recv()
         grads[:, rows:, :] = edge_in[...]
 
     @pl.when(me == members - 1)
@@ -478,9 +481,8 @@
     for which in range(3):
         outward_all(which).wait_send()
         homeward_all(which).wait_send()
+        homeward_top_all(which).wait_send()
     outward_top_all.wait_send()
-    homeward_top_all.wait_send()
-    homeward_last_all.wait_send()
     each_piece(lambda piece: part_out(piece, me).wait_send())
 
     @pl.when(me < pieces)
@@ -493,7 +495,8 @@
 
     @pl.when(me > 0)
     def _():
-        edge_copy.wait_send()
+        query_edge.wait_send()
+        other_edges.wait_send()
 
 
 def tables(members, rows):
@@ -507,26 +510,33 @@
 
     def split(matrix):
         high = matrix.astype(jnp.bfloat16)
-        return high, (matrix - high.astype(np.float64)).astype(jnp.bfloat16)
+        low = (matrix - high.astype(np.float64)).astype(jnp.bfloat16)
+        return np.concatenate([high, high, low])
 
     return (
         np.cos(coarse).astype(np.float32),
         np.sin(coarse).astype(np.float32),
         np.stack([np.cos(twist), np.sin(twist)]).astype(np.float32),
-        *split(forward),
-        *split(forward.T),
+        split(forward),
+        split(forward.T),
     )
 
 
 def hand_over(*refs):
-    sem = refs[8]
-    copies = [
-        pltpu.make_async_copy(source, target, sem.at[place])
-        for place, (source, target) in enumerate(zip(refs[:4], refs[4:8]))
+    sem = refs[12]
+    arrivals = [
+        pltpu.make_async_copy(refs[place], refs[8 + place], sem.at[0, place]) for place in range(4)
     ]
-    for copy in copies:
+    leaving = [
+        pltpu.make_async_copy(refs[8 + place], refs[4 + place], sem.at[1, place])
+        for place in range(4)
+    ]
+    for copy in arrivals:
         copy.start()
-    for copy in copies:
+    for arrival, copy in zip(arrivals, leaving):
+        arrival.wait()
+        copy.start()
+    for copy in leaving:
         copy.wait()
 
 
@@ -549,7 +559,7 @@
                 jax.ShapeDtypeStruct(short_weight.shape, f32),
                 jax.ShapeDtypeStruct((rows, width), f32),
             ),
-            in_specs=[vmem] * 4 + [smem] * 2 + [vmem] * 5,
+            in_specs=[vmem] * 4 + [smem] * 2 + [vmem] + [pl.BlockSpec(memory_space=pl.ANY)] * 2,
             out_specs=(vmem,) * 4,
             scratch_shapes=[
                 pltpu.VMEM((3, width, rows), f32),
@@ -558,11 +568,9 @@
                 wire,
                 pltpu.VMEM((members, 1, 384), f32),
                 wire,
-                pltpu.VMEM((members, 1, 256), f32),
-                pltpu.VMEM((members, 1, 128), f32),
+                pltpu.VMEM((3, members, 1, 128), f32),
                 wire,
-                pltpu.VMEM((members, 1, 256), f32),
-                pltpu.VMEM((members, 1, 128), f32),
+                pltpu.VMEM((3, members, 1, 128), f32),
                 pltpu.VMEM((members, chans, rows), f32),
                 pltpu.VMEM((3, members + 1, chans, 2 * rows), f32),
                 pltpu.VMEM((members + 1, chans, 2 * rows), f32),
@@ -581,16 +589,17 @@
                 dma((1,)),
                 dma((3,)),
                 dma((3,)),
-                dma((1,)),
-                dma((1,)),
-                dma((1,)),
-                dma((1,)),
+                dma((3,)),
+                dma((3,)),
                 dma((2,)),
-                dma((2,)),
+                dma((4,)),
                 dma((pieces,)),
                 dma((1,)),
                 dma((1,)),
                 dma((pieces,)),
+                pltpu.VMEM((6 * rows, 2 * rows), jnp.bfloat16),
+                pltpu.VMEM((6 * rows, 2 * rows), jnp.bfloat16),
+                dma((2,)),
             ],
             compiler_params=pltpu.CompilerParams(
                 collective_id=0, has_side_effects=True, vmem_limit_bytes=56 * 1024 * 1024
@@ -607,7 +616,7 @@
             out_shape=tuple(jax.ShapeDtypeStruct(r.shape, r.dtype) for r in results),
             in_specs=[anywhere] * 4,
             out_specs=(anywhere,) * 4,
-            scratch_shapes=[dma((4,))],
+            scratch_shapes=[pltpu.VMEM(r.shape, r.dtype) for r in results] + [dma((2, 4))],
             compiler_params=pltpu.CompilerParams(vmem_limit_bytes=60 * 1024 * 1024),
         )(*results)
     )

time: 108 us -> 58.9 us (0.55)
  Pallas kernels: 107 us -> 58.1 us
    pallas_call x1, Pallas kernels: 50.3 us -> 2.36 us  [on_device(): pl.pallas_call(hand_over, out_shape=tuple((jax.ShapeDtypeStruct(r.shape,...]
    pallas_call x1, Pallas kernels: 57.1 us -> 55.7 us  [on_device(): pl.pallas_call(functools.partial(hyena_kernel, members, norm), out_shape=...]
where the time goes in v3:
time: 58.9 us; the launch traced here: 58.7 us
  Pallas kernels  58.1 us (99%)
  between operations  0.64 us (1%)
    pallas_call x1, Pallas kernels, on_device(): pl.pallas_call(functools.partial(hyena_kernel, members, norm), out_shape=...  55.7 us
    pallas_call x1, Pallas kernels, on_device(): pl.pallas_call(hand_over, out_shape=tuple((jax.ShapeDtypeStruct(r.shape,...  2.36 us

profile of v3, /device:TPU:0, one launch (start us, length us, event | category | flops | bytes accessed | tf_op | source)
XLA Modules:
  0.0 58.7 jit_solution(5601286874909478781)
XLA Ops:
  0.6 55.7 %shard_map.120 = (bf16[256,512]{1,0:T(8,128)(2,1)}, bf16[3,256,512]{2,1,0:T(8,128)(2,1)}, f32[3,7,512]{2,1,0:T(8,128)}, f32[256,512]{1,0:T(8,128)}) custom-call(bf16[3,256,512]{2,1,0:T(8,128)(2,1)} %streams_ref.1, f32[3,7,512]{2,1,0:T(8,128)} %weight_ref.1, f32[256,512]{1,0:T(8,128)} %filt_ref.1, bf16[256,512]{1,0:T(8,128)(2,1)} %cot_ref.1, ...), custom_call_target="tpu_custom_call" | custom-call | tf_op jit(solution)/shard_map/pallas_call | solution.py:554
  56.4 2.4 %shard_map.121 = (bf16[256,512]{1,0:T(8,128)(2,1)}, bf16[3,256,512]{2,1,0:T(8,128)(2,1)}, f32[3,7,512]{2,1,0:T(8,128)}, f32[256,512]{1,0:T(8,128)}) custom-call(bf16[256,512]{1,0:T(8,128)(2,1)} %get-tuple-element.8.refs_0_, bf16[3,256,512]{2,1,0:T(8,128)(2,1)} %get-tuple-element.9.refs_1_, f32[3,7,512]{2,1,0:T(8,128)} %get-tuple-element.10.refs_2_, ...), custom_call_target="tpu_custom_call" | custom-call | tf_op jit(solution)/shard_map/pallas_call | solution.py:614

commit v4 on v3

--- a/solution.py
+++ b/solution.py
@@ -90,6 +90,11 @@
         )
 
     def others(body):
+        if members <= 16:
+            for step in range(1, members):
+                body(lax.rem(me + step, members))
+            return
+
         def one(step, carry):
             body(lax.rem(me + step, members))
             return carry
@@ -223,13 +228,13 @@
         return carry
 
     lax.fori_loop(0, chunks, featurize, 0)
+    turned[2] = grads[1, :rows, :].T
+    pack_all(2)
+    others(lambda other: outward(2, other, me).start())
     turned[1] = grads[0, :rows, :].T
-    turned[2] = grads[1, :rows, :].T
     pack_all(1)
-    pack_all(2)
     others(lambda other: outward_top(other, me).start())
     others(lambda other: outward(1, other, me).start())
-    others(lambda other: outward(2, other, me).start())
     got[1, me] = packed[1, me]
     got[2, me] = packed[2, me]
     got_tops[me] = tops[me]
@@ -340,11 +345,11 @@
 
     fwd_copy.wait()
     forward(0)
+    forward(2)
+    inv_copy.wait()
+    inverse(1, 0, 2, -1.0)
     forward(1)
-    inv_copy.wait()
     inverse(0, 0, 1, 1.0)
-    forward(2)
-    inverse(1, 0, 2, -1.0)
     inverse(2, 1, 2, -1.0)
 
     def settle(which):
@@ -402,28 +407,6 @@
         for tile in range(lane_tiles):
             parts[which * lane_tiles + tile] = block[:, tile * 128 : tile * 128 + 128]
 
-    settle(0)
-    grads[0, :rows, :] = turned[0].T
-    lax.fori_loop(0, chunks, gate_query, 0)
-    edge_out[0] = grads[0, :edge, :]
-
-    @pl.when(me > 0)
-    def _():
-        query_edge.start()
-
-    all_taps(0)
-    settle(1)
-    grads[1, :rows, :] = turned[1].T
-    lax.fori_loop(0, chunks, gate_others, 0)
-    edge_out[1:] = grads[1:, :edge, :]
-
-    @pl.when(me > 0)
-    def _():
-        other_edges.start()
-
-    all_taps(1)
-    all_taps(2)
-
     def each_piece(body):
         def one(piece, carry):
             @pl.when(piece != me)
@@ -434,29 +417,59 @@
 
         lax.fori_loop(0, pieces, one, 0)
 
-    each_piece(lambda piece: part_out(piece, me).start())
-
-    @pl.when(me < members - 1)
-    def _():
-        query_edge.wait_recv()
-        other_edges.wait_recv()
-        grads[:, rows:, :] = edge_in[...]
-
-    @pl.when(me == members - 1)
-    def _():
-        grads[:, rows:, :] = jnp.zeros((3, edge, width), f32)
-
-    def back_taps(step, carry):
-        start = pl.multiple_of(step * step_rows, step_rows)
-        for which in range(3):
+    def back_taps(which):
+        def one(step, carry):
+            start = pl.multiple_of(step * step_rows, step_rows)
             window = grads[which, pl.ds(start, step_rows + edge), :]
             total = weight_ref[which, 0:1, :] * window[:step_rows]
             for tap in range(1, taps):
                 total = total + weight_ref[which, tap : tap + 1, :] * window[tap : tap + step_rows]
             stream_grad_ref[which, pl.ds(start, step_rows), :] = total.astype(jnp.bfloat16)
-        return carry
-
-    lax.fori_loop(0, chunks, back_taps, 0)
+            return carry
+
+        lax.fori_loop(0, chunks, one, 0)
+
+    @pl.when(me == members - 1)
+    def _():
+        grads[:, rows:, :] = jnp.zeros((3, edge, width), f32)
+
+    settle(1)
+    grads[1, :rows, :] = turned[1].T
+    lax.fori_loop(0, chunks, gate_others, 0)
+    edge_out[1:] = grads[1:, :edge, :]
+
+    @pl.when(me > 0)
+    def _():
+        other_edges.start()
+
+    all_taps(1)
+    all_taps(2)
+
+    @pl.when(me < members - 1)
+    def _():
+        other_edges.wait_recv()
+        grads[1:, rows:, :] = edge_in[1:]
+
+    back_taps(1)
+    back_taps(2)
+    settle(0)
+    grads[0, :rows, :] = turned[0].T
+    lax.fori_loop(0, chunks, gate_query, 0)
+    edge_out[0] = grads[0, :edge, :]
+
+    @pl.when(me > 0)
+    def _():
+        query_edge.start()
+
+    all_taps(0)
+    each_piece(lambda piece: part_out(piece, me).start())
+
+    @pl.when(me < members - 1)
+    def _():
+        query_edge.wait_recv()
+        grads[0, rows:, :] = edge_in[0]
+
+    back_taps(0)
 
     @pl.when(me < pieces)
     def _():

time: 58.9 us -> 63.7 us (1.081)
  Pallas kernels: 58.1 us -> 62.9 us
    pallas_call x1, Pallas kernels: 55.7 us -> 60.5 us  [on_device(): pl.pallas_call(functools.partial(hyena_kernel, members, norm), out_shape=...]
where the time goes in v4:
time: 63.7 us; the launch traced here: 63.5 us
  Pallas kernels  62.9 us (99%)
  between operations  0.64 us (1%)
    pallas_call x1, Pallas kernels, on_device(): pl.pallas_call(functools.partial(hyena_kernel, members, norm), out_shape=...  60.5 us
    pallas_call x1, Pallas kernels, on_device(): pl.pallas_call(hand_over, out_shape=tuple((jax.ShapeDtypeStruct(r.shape,...  2.36 us

profile of v4, /device:TPU:0, one launch (start us, length us, event | category | flops | bytes accessed | tf_op | source)
XLA Modules:
  0.0 63.5 jit_solution(1339083489230313456)
XLA Ops:
  0.6 60.5 %shard_map.120 = (bf16[256,512]{1,0:T(8,128)(2,1)}, bf16[3,256,512]{2,1,0:T(8,128)(2,1)}, f32[3,7,512]{2,1,0:T(8,128)}, f32[256,512]{1,0:T(8,128)}) custom-call(bf16[3,256,512]{2,1,0:T(8,128)(2,1)} %streams_ref.1, f32[3,7,512]{2,1,0:T(8,128)} %weight_ref.1, f32[256,512]{1,0:T(8,128)} %filt_ref.1, bf16[256,512]{1,0:T(8,128)(2,1)} %cot_ref.1, ...), custom_call_target="tpu_custom_call" | custom-call | tf_op jit(solution)/shard_map/pallas_call | solution.py:567
  61.2 2.4 %shard_map.121 = (bf16[256,512]{1,0:T(8,128)(2,1)}, bf16[3,256,512]{2,1,0:T(8,128)(2,1)}, f32[3,7,512]{2,1,0:T(8,128)}, f32[256,512]{1,0:T(8,128)}) custom-call(bf16[256,512]{1,0:T(8,128)(2,1)} %get-tuple-element.8.refs_0_, bf16[3,256,512]{2,1,0:T(8,128)(2,1)} %get-tuple-element.9.refs_1_, f32[3,7,512]{2,1,0:T(8,128)} %get-tuple-element.10.refs_2_, ...), custom_call_target="tpu_custom_call" | custom-call | tf_op jit(solution)/shard_map/pallas_call | solution.py:627

commit v5 on v4

--- a/solution.py
+++ b/solution.py
@@ -68,7 +68,7 @@
     fwd_any, inv_any,
     hyena_ref, stream_grad_ref, short_ref, filter_grad_ref,
     turned, packed, tops, got, got_tops, back, back_tops, home, home_tops,
-    waves, spectra, work, features, extended, grads, halo, edge_out, edge_in, parts, gathered, sums,
+    waves, spectra, work, folded, features, extended, grads, halo, edge_out, edge_in, parts, gathered, sums,
     send_sem, recv_sem, top_send, top_recv, back_send, back_recv, back_top_send, back_top_recv,
     halo_sem, edge_sem, part_send, part_recv, sum_send, sum_recv,
     fwd_ref, inv_ref, table_sem,
@@ -78,6 +78,7 @@
     rows, width = filt_ref.shape
     chans = width // members
     half = members // 2
+    quarter = members // 4
     taps = weight_ref.shape[1]
     lane_tiles = width // 128
     pieces = 3 * lane_tiles
@@ -107,9 +108,10 @@
             send_sem.at[which], recv_sem.at[which], other,
         )
 
-    def outward_top(other, source):
-        return remote(
-            tops.at[other], got_tops.at[source], top_send.at[0], top_recv.at[0], other
+    def outward_top(which, other, source):
+        return remote(
+            tops.at[which, other], got_tops.at[which, source],
+            top_send.at[which], top_recv.at[which], other,
         )
 
     def homeward(which, other, source):
@@ -147,9 +149,12 @@
             back.at[which, most], home.at[which, most], back_send.at[which], back_recv.at[which], near
         )
 
-    outward_top_all = remote(
-        tops.at[most], got_tops.at[most], top_send.at[0], top_recv.at[0], near
-    )
+    def outward_top_all(which):
+        return remote(
+            tops.at[which, most], got_tops.at[which, most],
+            top_send.at[which], top_recv.at[which], near,
+        )
+
     def homeward_top_all(which):
         return remote(
             back_tops.at[which, most], home_tops.at[which, most],
@@ -180,7 +185,7 @@
         values = turned[which, other * chans : other * chans + chans, :]
         top = row_top(values)
         packed[which, other] = encode(values, top)
-        tops[other, :, which * 128 : which * 128 + 128] = to_lanes(top)
+        tops[which, other] = to_lanes(top)
 
     def pack_all(which):
         for other in range(members):
@@ -198,8 +203,13 @@
     def _():
         halo_out.start()
 
-    others(lambda other: outward(0, other, me).start())
-    got[0, me] = packed[0, me]
+    def send_out(which):
+        others(lambda other: outward_top(which, other, me).start())
+        others(lambda other: outward(which, other, me).start())
+        got[which, me] = packed[which, me]
+        got_tops[which, me] = tops[which, me]
+
+    send_out(0)
 
     for which in range(3):
         extended[which, edge:, :] = streams_ref[which].astype(f32)
@@ -230,37 +240,33 @@
     lax.fori_loop(0, chunks, featurize, 0)
     turned[2] = grads[1, :rows, :].T
     pack_all(2)
-    others(lambda other: outward(2, other, me).start())
+    send_out(2)
     turned[1] = grads[0, :rows, :].T
     pack_all(1)
-    others(lambda other: outward_top(other, me).start())
-    others(lambda other: outward(1, other, me).start())
-    got[1, me] = packed[1, me]
-    got[2, me] = packed[2, me]
-    got_tops[me] = tops[me]
-    outward_top_all.wait_recv()
+    send_out(1)
 
     height = (members + 1) * chans
 
     def forward(which):
+        outward_top_all(which).wait_recv()
         outward_all(which).wait_recv()
         for source in range(members):
-            top = to_column(got_tops[source, :, which * 128 : which * 128 + 128], chans)
+            top = to_column(got_tops[which, source], chans)
             if which == 0:
                 top = top * norm
             waves[source] = decode(got[which, source], top)
 
         def coarse(freq, carry):
             sides = []
-            for parity in range(2):
+            for residue in range(4):
                 real = jnp.zeros((chans, rows), f32)
                 imag = jnp.zeros((chans, rows), f32)
-                for block in range(parity, members, 2):
+                for block in range(residue, members, 4):
                     value = waves[block]
                     real = real + cos_ref[freq, block] * value
                     imag = imag - sin_ref[freq, block] * value
                 sides.append((real, imag))
-            (even_r, even_i), (odd_r, odd_i) = sides
+            (ar, ai), (br, bi), (cr, ci), (dr, di) = sides
 
             def put(place, real, imag):
                 cosine = twist_ref[0, pl.ds(place, 1), :]
@@ -268,11 +274,13 @@
                 spectra[which, place, :, :rows] = real * cosine + imag * sine
                 spectra[which, place, :, rows:] = imag * cosine - real * sine
 
-            put(members - freq, even_r - odd_r, odd_i - even_i)
-            put(freq, even_r + odd_r, even_i + odd_i)
+            put(freq, (ar + cr) + (br + dr), (ai + ci) + (bi + di))
+            put(members - freq, (ar + cr) - (br + dr), (bi + di) - (ai + ci))
+            put(half - freq, (ar - cr) - (bi - di), (ci - ai) - (br - dr))
+            put(half + freq, (ar - cr) + (bi - di), (ai - ci) - (br - dr))
             return carry
 
-        lax.fori_loop(0, half + 1, coarse, 0)
+        lax.fori_loop(0, quarter + 1, coarse, 0)
         flat = spectra[which].reshape(height, 2 * rows)
         spectra[which] = three_products(flat, fwd_ref).reshape(
             members + 1, chans, 2 * rows
@@ -298,34 +306,40 @@
                 imag = work[place, :, rows:]
                 return real * cosine - imag * sine, imag * cosine + real * sine
 
-            lr, li = turn(freq)
-            ur, ui = turn(members - freq)
-            ones = jnp.where(freq == half, 0.0, 1.0)
-            weight = jnp.where(freq == 0, 1.0, 2.0) * (scale / (2.0 * members * rows))
-            work[freq, :, :rows] = weight * (lr + ones * ur)
-            work[freq, :, rows:] = weight * (li - ones * ui)
-
-            @pl.when(freq < half)
-            def _():
-                work[members - freq, :, :rows] = weight * (lr - ur)
-                work[members - freq, :, rows:] = weight * (li + ui)
-
+            unit = scale / (2.0 * members * rows)
+            first, last = freq == 0, freq == quarter
+            outer = jnp.where(first, unit, 2.0 * unit)
+            inner = jnp.where(last, 0.0, 2.0 * unit)
+            upper = jnp.where(first, 0.0, inner)
+            ar, ai = [outer * part for part in turn(freq)]
+            br, bi = [outer * part for part in turn(members - freq)]
+            cr, ci = [inner * part for part in turn(half - freq)]
+            dr, di = [upper * part for part in turn(half + freq)]
+            sums_r, diff_r = ar + br, ar - br
+            sums_i, diff_i = ai + bi, ai - bi
+            folded[0, freq, :, :rows] = sums_r + (cr + dr)
+            folded[0, freq, :, rows:] = diff_i - (ci - di)
+            folded[1, freq, :, :rows] = diff_r - (ci + di)
+            folded[1, freq, :, rows:] = sums_i - (cr - dr)
+            folded[2, freq, :, :rows] = sums_r - (cr + dr)
+            folded[2, freq, :, rows:] = diff_i + (ci - di)
+            folded[3, freq, :, :rows] = diff_r + (ci + di)
+            folded[3, freq, :, rows:] = sums_i + (cr - dr)
             return carry
 
         scale = norm if which == 2 else 1.0
-        lax.fori_loop(0, half + 1, untwist, 0)
-
-        def total_of(block, odd):
+        lax.fori_loop(0, quarter + 1, untwist, 0)
+
+        def total_of(block, residue):
             total = jnp.zeros((chans, rows), f32)
-            for freq in range(half + 1):
-                place = members - freq if odd else freq
-                total = total + cos_ref[freq, block] * work[place, :, :rows]
-                total = total - sin_ref[freq, block] * work[place, :, rows:]
+            for freq in range(quarter + 1):
+                total = total + cos_ref[freq, block] * folded[residue, freq, :, :rows]
+                total = total - sin_ref[freq, block] * folded[residue, freq, :, rows:]
             return total
 
         def finish(step, carry):
             blocks = [step * 4 + place for place in range(4)]
-            totals = [total_of(block, place % 2 == 1) for place, block in enumerate(blocks)]
+            totals = [total_of(block, place) for place, block in enumerate(blocks)]
             for block, total in zip(blocks, totals):
                 top = row_top(total)
                 back[which, block] = encode(total, top)
@@ -495,7 +509,7 @@
         outward_all(which).wait_send()
         homeward_all(which).wait_send()
         homeward_top_all(which).wait_send()
-    outward_top_all.wait_send()
+        outward_top_all(which).wait_send()
     each_piece(lambda piece: part_out(piece, me).wait_send())
 
     @pl.when(me < pieces)
@@ -577,9 +591,9 @@
             scratch_shapes=[
                 pltpu.VMEM((3, width, rows), f32),
                 wire,
-                pltpu.VMEM((members, 1, 384), f32),
+                pltpu.VMEM((3, members, 1, 128), f32),
                 wire,
-                pltpu.VMEM((members, 1, 384), f32),
+                pltpu.VMEM((3, members, 1, 128), f32),
                 wire,
                 pltpu.VMEM((3, members, 1, 128), f32),
                 wire,
@@ -587,6 +601,7 @@
                 pltpu.VMEM((members, chans, rows), f32),
                 pltpu.VMEM((3, members + 1, chans, 2 * rows), f32),
                 pltpu.VMEM((members + 1, chans, 2 * rows), f32),
+                pltpu.VMEM((4, members // 4 + 1, chans, 2 * rows), f32),
                 pltpu.VMEM((3, rows, width), f32),
                 pltpu.VMEM((3, rows + edge, width), f32),
                 pltpu.VMEM((3, rows + edge, width), f32),
@@ -598,8 +613,8 @@
                 pltpu.VMEM((pieces, 8, 128), f32),
                 dma((3,)),
                 dma((3,)),
-                dma((1,)),
-                dma((1,)),
+                dma((3,)),
+                dma((3,)),
                 dma((3,)),
                 dma((3,)),
                 dma((3,)),

time: 63.7 us -> 57.7 us (0.906)
  Pallas kernels: 62.9 us -> 56.9 us
    pallas_call x1, Pallas kernels: 60.5 us -> 54.5 us  [on_device(): pl.pallas_call(functools.partial(hyena_kernel, members, norm), out_shape=...]
where the time goes in v5:
time: 57.7 us; the launch traced here: 57.5 us
  Pallas kernels  56.9 us (99%)
  between operations  0.64 us (1%)
    pallas_call x1, Pallas kernels, on_device(): pl.pallas_call(functools.partial(hyena_kernel, members, norm), out_shape=...  54.5 us
    pallas_call x1, Pallas kernels, on_device(): pl.pallas_call(hand_over, out_shape=tuple((jax.ShapeDtypeStruct(r.shape,...  2.36 us

profile of v5, /device:TPU:0, one launch (start us, length us, event | category | flops | bytes accessed | tf_op | source)
XLA Modules:
  0.0 57.5 jit_solution(18009538780294495296)
XLA Ops:
  0.6 54.5 %shard_map.120 = (bf16[256,512]{1,0:T(8,128)(2,1)}, bf16[3,256,512]{2,1,0:T(8,128)(2,1)}, f32[3,7,512]{2,1,0:T(8,128)}, f32[256,512]{1,0:T(8,128)}) custom-call(bf16[3,256,512]{2,1,0:T(8,128)(2,1)} %streams_ref.1, f32[3,7,512]{2,1,0:T(8,128)} %weight_ref.1, f32[256,512]{1,0:T(8,128)} %filt_ref.1, bf16[256,512]{1,0:T(8,128)(2,1)} %cot_ref.1, ...), custom_call_target="tpu_custom_call" | custom-call | tf_op jit(solution)/shard_map/pallas_call | solution.py:581
  55.2 2.4 %shard_map.121 = (bf16[256,512]{1,0:T(8,128)(2,1)}, bf16[3,256,512]{2,1,0:T(8,128)(2,1)}, f32[3,7,512]{2,1,0:T(8,128)}, f32[256,512]{1,0:T(8,128)}) custom-call(bf16[256,512]{1,0:T(8,128)(2,1)} %get-tuple-element.8.refs_0_, bf16[3,256,512]{2,1,0:T(8,128)(2,1)} %get-tuple-element.9.refs_1_, f32[3,7,512]{2,1,0:T(8,128)} %get-tuple-element.10.refs_2_, ...), custom_call_target="tpu_custom_call" | custom-call | tf_op jit(solution)/shard_map/pallas_call | solution.py:642

commit v6 on v5

--- a/solution.py
+++ b/solution.py
@@ -9,8 +9,8 @@
 from jax.experimental.pallas import tpu as pltpu
 from jax.sharding import PartitionSpec as P
 
-span = 250.0
-half_span = 125.0
+span = 250.0 * math.log(2.0)
+half_span = 0.5 * span
 tiny = 1e-30
 edge = 8
 step_rows = 32
@@ -19,13 +19,13 @@
 
 def encode(values, top):
     power = jnp.abs(values) * (span / top) - half_span
-    code = jnp.exp2(power)
+    code = jnp.exp(power)
     return jnp.where(values < 0.0, -code, code).astype(jnp.bfloat16)
 
 
 def decode(code, top):
     code = code.astype(f32)
-    size = (jnp.log2(jnp.abs(code)) + half_span) * (top * (1.0 / span))
+    size = (jnp.log(jnp.abs(code)) + half_span) * (top * (1.0 / span))
     return jnp.where(code < 0.0, -size, size)
 
 
@@ -214,18 +214,9 @@
     for which in range(3):
         extended[which, edge:, :] = streams_ref[which].astype(f32)
 
-    @pl.when(me > 0)
-    def _():
-        halo_out.wait_recv()
-        for which in range(3):
-            extended[which, :edge, :] = halo[which].astype(f32)[16 - edge :]
-
-    @pl.when(me == 0)
-    def _():
-        extended[:, :edge, :] = jnp.zeros((3, edge, width), f32)
-
     def featurize(step, carry):
-        start = pl.multiple_of(step * step_rows, step_rows)
+        start = step * step_rows
+        start = start if isinstance(step, int) else pl.multiple_of(start, step_rows)
         query, key, value = [
             feature_rows(extended, weight_ref, which, start) for which in range(3)
         ]
@@ -237,7 +228,19 @@
         grads[1, here, :] = cot_ref[here, :].astype(f32) * query
         return carry
 
-    lax.fori_loop(0, chunks, featurize, 0)
+    lax.fori_loop(1, chunks, featurize, 0)
+
+    @pl.when(me > 0)
+    def _():
+        halo_out.wait_recv()
+        for which in range(3):
+            extended[which, :edge, :] = halo[which].astype(f32)[16 - edge :]
+
+    @pl.when(me == 0)
+    def _():
+        extended[:, :edge, :] = jnp.zeros((3, edge, width), f32)
+
+    featurize(0, 0)
     turned[2] = grads[1, :rows, :].T
     pack_all(2)
     send_out(2)
@@ -431,7 +434,7 @@
 
         lax.fori_loop(0, pieces, one, 0)
 
-    def back_taps(which):
+    def back_taps(which, begin, end):
         def one(step, carry):
             start = pl.multiple_of(step * step_rows, step_rows)
             window = grads[which, pl.ds(start, step_rows + edge), :]
@@ -441,7 +444,7 @@
             stream_grad_ref[which, pl.ds(start, step_rows), :] = total.astype(jnp.bfloat16)
             return carry
 
-        lax.fori_loop(0, chunks, one, 0)
+        lax.fori_loop(begin, end, one, 0)
 
     @pl.when(me == members - 1)
     def _():
@@ -458,14 +461,16 @@
 
     all_taps(1)
     all_taps(2)
+    back_taps(1, 0, chunks - 1)
+    back_taps(2, 0, chunks - 1)
 
     @pl.when(me < members - 1)
     def _():
         other_edges.wait_recv()
         grads[1:, rows:, :] = edge_in[1:]
 
-    back_taps(1)
-    back_taps(2)
+    back_taps(1, chunks - 1, chunks)
+    back_taps(2, chunks - 1, chunks)
     settle(0)
     grads[0, :rows, :] = turned[0].T
     lax.fori_loop(0, chunks, gate_query, 0)
@@ -477,13 +482,14 @@
 
     all_taps(0)
     each_piece(lambda piece: part_out(piece, me).start())
+    back_taps(0, 0, chunks - 1)
 
     @pl.when(me < members - 1)
     def _():
         query_edge.wait_recv()
         grads[0, rows:, :] = edge_in[0]
 
-    back_taps(0)
+    back_taps(0, chunks - 1, chunks)
 
     @pl.when(me < pieces)
     def _():

time: 57.7 us -> 57.7 us (level)
  no operation moved by 1% of the time
where the time goes in v6:
time: 57.7 us; the launch traced here: 57.5 us
  Pallas kernels  56.9 us (99%)
  between operations  0.64 us (1%)
    pallas_call x1, Pallas kernels, on_device(): pl.pallas_call(functools.partial(hyena_kernel, members, norm), out_shape=...  54.5 us
    pallas_call x1, Pallas kernels, on_device(): pl.pallas_call(hand_over, out_shape=tuple((jax.ShapeDtypeStruct(r.shape,...  2.36 us

profile of v6, /device:TPU:0, one launch (start us, length us, event | category | flops | bytes accessed | tf_op | source)
XLA Modules:
  0.0 57.5 jit_solution(10581266577375387239)
XLA Ops:
  0.6 54.5 %shard_map.120 = (bf16[256,512]{1,0:T(8,128)(2,1)}, bf16[3,256,512]{2,1,0:T(8,128)(2,1)}, f32[3,7,512]{2,1,0:T(8,128)}, f32[256,512]{1,0:T(8,128)}) custom-call(bf16[3,256,512]{2,1,0:T(8,128)(2,1)} %streams_ref.1, f32[3,7,512]{2,1,0:T(8,128)} %weight_ref.1, f32[256,512]{1,0:T(8,128)} %filt_ref.1, bf16[256,512]{1,0:T(8,128)(2,1)} %cot_ref.1, ...), custom_call_target="tpu_custom_call" | custom-call | tf_op jit(solution)/shard_map/pallas_call | solution.py:587
  55.1 2.4 %shard_map.121 = (bf16[256,512]{1,0:T(8,128)(2,1)}, bf16[3,256,512]{2,1,0:T(8,128)(2,1)}, f32[3,7,512]{2,1,0:T(8,128)}, f32[256,512]{1,0:T(8,128)}) custom-call(bf16[256,512]{1,0:T(8,128)(2,1)} %get-tuple-element.8.refs_0_, bf16[3,256,512]{2,1,0:T(8,128)(2,1)} %get-tuple-element.9.refs_1_, f32[3,7,512]{2,1,0:T(8,128)} %get-tuple-element.10.refs_2_, ...), custom_call_target="tpu_custom_call" | custom-call | tf_op jit(solution)/shard_map/pallas_call | solution.py:648
